TPU v7x, 256 devices: a whole 4x4x8 slice. The times are simulated.
256 devices in a mesh: context: 32 (over x, y, z_lo), tensor: 8 (over z_hi, core).
Axes of the slice: x: 4, y: 4, z: 8 (z_hi: 4, z_lo: 2; z = z_hi * 2 + z_lo), core: 2. Of those that a mesh axis runs over, the one named last changes fastest.
Arguments:
- query_proj: bfloat16 [16384, 4096], P('context', 'tensor'), may hold values from -6 to 6
- key_proj: bfloat16 [16384, 4096], P('context', 'tensor'), may hold values from -6 to 6
- value_proj: bfloat16 [16384, 4096], P('context', 'tensor'), may hold values from -6 to 6
- filter_gains: float32 [4096, 16], P('tensor'), may hold values from -3 to 3
- log_rates: float32 [4096, 16], P('tensor'), may hold values from -12 to -0.5
- out_weight: bfloat16 [4096, 4096], P('tensor', 'context'), may hold values from -0.09375 to 0.09375
- grad_out: bfloat16 [16384, 4096], P('context', 'tensor'), may hold values from -6 to 6
Outputs:
- grad_query: bfloat16 [16384, 4096], P('context', 'tensor')
- grad_key: bfloat16 [16384, 4096], P('context', 'tensor')
- grad_value: bfloat16 [16384, 4096], P('context', 'tensor')
- grad_gains: float32 [4096, 16], P('tensor')
- grad_log_rates: float32 [4096, 16], P('tensor')
- grad_out_weight: float32 [4096, 4096], P('tensor', 'context')
All inputs are finite; a program needn't handle non-finite values.
Results may differ from a plain program's by a relative error of at most 0.03.
Values may be sent and summed in bfloat16 or wider, within the bound.
A program may use at most 128 MiB of HBM per device.

v0:
```python
import math

import jax
import jax.numpy as jnp
from jax import lax
from jax.sharding import PartitionSpec as P

FFT_BLOCK = 1024


TWO_PI = 2.0 * math.pi


def angle_grid(first_vals, second_vals, period):
    product = first_vals[:, None] * second_vals[None, :] % period
    return product.astype(jnp.float32) * (TWO_PI / period)


def front_table(block_len):
    angles = angle_grid(
        jnp.arange(block_len, dtype=jnp.int32),
        jnp.arange(block_len // 2, dtype=jnp.int32),
        block_len,
    )
    return jnp.concatenate([jnp.cos(angles), -jnp.sin(angles)], axis=0)


def inner_table(inner_len, sign_value):
    angles = angle_grid(
        jnp.arange(inner_len, dtype=jnp.int32), jnp.arange(inner_len, dtype=jnp.int32), inner_len
    )
    cosines = jnp.cos(angles)
    sine_vals = sign_value * jnp.sin(angles)
    return jnp.stack([jnp.stack([cosines, sine_vals]), jnp.stack([-sine_vals, cosines])])


def end_table(block_len):
    angles = angle_grid(
        jnp.arange(block_len // 2, dtype=jnp.int32),
        jnp.arange(block_len, dtype=jnp.int32),
        block_len,
    )
    return jnp.concatenate([jnp.cos(angles), -jnp.sin(angles)], axis=1)


def first_section(gathered, front_rows, turn_cos, turn_sin):
    span_half, inner_local, chan_count = gathered.shape
    flat_grid = gathered.reshape(span_half, inner_local * chan_count)
    mixed_rows = jnp.dot(front_rows, flat_grid, preferred_element_type=jnp.float32)
    mixed_rows = mixed_rows.reshape(2, front_rows.shape[0] // 2, inner_local, chan_count)
    real_part = mixed_rows[0] * turn_cos[:, :, None] + mixed_rows[1] * turn_sin[:, :, None]
    imag_part = mixed_rows[1] * turn_cos[:, :, None] - mixed_rows[0] * turn_sin[:, :, None]
    stacked = jnp.stack([real_part, imag_part])
    return stacked.astype(jnp.bfloat16)


def second_section(moved_cols, inner_rows):
    spectrum = jnp.einsum(
        "xykn,yanc->xakc", inner_rows, moved_cols, preferred_element_type=jnp.float32
    )
    return spectrum.astype(jnp.bfloat16)


def back_section(spectrum, inner_rows, back_cos, back_sin):
    summed = jnp.einsum("xynk,yakc->xanc", inner_rows, spectrum, preferred_element_type=jnp.float32)
    real_part = summed[0] * back_cos[:, :, None] - summed[1] * back_sin[:, :, None]
    imag_part = summed[1] * back_cos[:, :, None] + summed[0] * back_sin[:, :, None]
    return jnp.stack([real_part, imag_part]).astype(jnp.bfloat16)


def last_section(moved_cols, end_rows, scale_val):
    inner_local = moved_cols.shape[2]
    chan_count = moved_cols.shape[3]
    flat_grid = moved_cols.reshape(
        moved_cols.shape[0] * moved_cols.shape[1], inner_local * chan_count
    )
    values = jnp.dot(end_rows, flat_grid, preferred_element_type=jnp.float32) * scale_val
    return values.reshape(end_rows.shape[0], inner_local, chan_count).astype(jnp.bfloat16)


def complex_times(left_spec, right_spec):
    left_re = left_spec[0]
    left_im = left_spec[1]
    right_re = right_spec[0].astype(jnp.float32)
    right_im = right_spec[1].astype(jnp.float32)
    real_part = left_re * right_re - left_im * right_im
    imag_part = left_re * right_im + left_im * right_re
    return jnp.stack([real_part, imag_part]).astype(jnp.bfloat16)


def conj_times(left_spec, right_spec):
    left_re = left_spec[0].astype(jnp.float32)
    left_im = left_spec[1].astype(jnp.float32)
    right_re = right_spec[0].astype(jnp.float32)
    right_im = right_spec[1].astype(jnp.float32)
    real_part = left_re * right_re + left_im * right_im
    imag_part = left_re * right_im - left_im * right_re
    return jnp.stack([real_part, imag_part]).astype(jnp.bfloat16)


def closed_spectrum(filter_gains, decay_rates, freq_ids, inner_len, full_len, seq_len):
    freq_grid = freq_ids[:, None] + FFT_BLOCK * jnp.arange(inner_len, dtype=jnp.int32)[None, :]
    theta_grid = freq_grid.astype(jnp.float32) * (TWO_PI / full_len)
    parity = (1.0 - 2.0 * (freq_ids % 2).astype(jnp.float32))[:, None, None, None]
    half_sine = jnp.sin(0.5 * theta_grid)[:, :, None, None]
    full_sine = jnp.sin(theta_grid)[:, :, None, None]
    mode_amps = (filter_gains * jnp.sqrt(2.0 * decay_rates))[None, None]
    rate_grid = decay_rates[None, None]
    step_decay = jnp.exp(-rate_grid)
    tail_decay = jnp.exp(-rate_grid * seq_len)
    den_real = -jnp.expm1(-rate_grid) + 2.0 * step_decay * half_sine * half_sine
    den_imag = step_decay * full_sine
    magnitude = den_real * den_real + den_imag * den_imag
    numer_scale = mode_amps * (1.0 - tail_decay * parity) / magnitude
    real_acc = jnp.sum(numer_scale * den_real, axis=3)
    imag_acc = -jnp.sum(numer_scale * den_imag, axis=3)
    return jnp.stack([real_acc, imag_acc])


def filter_terms(kernel_rows, kernel_times, decay_rates, filter_gains):
    kernel_real = kernel_rows.astype(jnp.float32)
    mode_basis = jnp.sqrt(2.0 * decay_rates)[None] * jnp.exp(
        -decay_rates[None] * kernel_times[:, None, None]
    )
    weighted = kernel_real[:, :, None] * mode_basis
    gain_sum = jnp.sum(weighted, axis=0)
    rate_sum = (
        jnp.sum(weighted * (0.5 - decay_rates[None] * kernel_times[:, None, None]), axis=0)
        * filter_gains
    )
    return (gain_sum, rate_sum)


def on_device(query_proj, key_proj, value_proj, filter_gains, log_rates, out_weight, grad_out):
    ctx_size = lax.axis_size("context")
    ctx_index = lax.axis_index("context")
    row_count, chan_count = query_proj.shape
    block_len = FFT_BLOCK
    half_len = block_len // 2
    seq_len = row_count * ctx_size
    full_len = 2 * seq_len
    inner_len = full_len // block_len
    inner_local = inner_len // ctx_size
    block_local = block_len // ctx_size
    half_local = half_len // ctx_size
    norm_scale = 1.0 / math.sqrt(seq_len)
    front_real = front_table(block_len)
    front_half = front_real.astype(jnp.bfloat16)
    inner_fwd = inner_table(inner_len, 1.0)
    inner_fwd_half = inner_fwd.astype(jnp.bfloat16)
    inner_back_half = inner_table(inner_len, -1.0).astype(jnp.bfloat16)
    end_half = end_table(block_len).astype(jnp.bfloat16)
    decay_rates = jnp.exp(log_rates)
    time_ids = (ctx_index * row_count + jnp.arange(row_count, dtype=jnp.int32)).astype(jnp.float32)
    gathered_out = lax.all_gather(grad_out, "tensor", axis=1, tiled=True)
    signal_in = (key_proj.astype(jnp.float32) * value_proj.astype(jnp.float32)).astype(jnp.bfloat16)
    column_ids = ctx_index * inner_local + jnp.arange(inner_local, dtype=jnp.int32)
    turn_angles = angle_grid(jnp.arange(block_len, dtype=jnp.int32), column_ids, full_len)
    turn_cos = jnp.cos(turn_angles)
    turn_sin = jnp.sin(turn_angles)
    freq_ids = ctx_index * block_local + jnp.arange(block_local, dtype=jnp.int32)
    back_angles = angle_grid(freq_ids, jnp.arange(inner_len, dtype=jnp.int32), full_len)
    back_cos = jnp.cos(back_angles)
    back_sin = jnp.sin(back_angles)

    def forward_signal(signal):
        grid_rows = signal.reshape(half_local, inner_len, chan_count)
        moved_rows = lax.all_to_all(grid_rows, "context", split_axis=1, concat_axis=0, tiled=True)
        turned = first_section(moved_rows, front_half, turn_cos, turn_sin)
        moved_cols = lax.all_to_all(turned, "context", split_axis=1, concat_axis=2, tiled=True)
        return second_section(moved_cols, inner_fwd_half)

    signal_spec = forward_signal(signal_in)
    filter_spec = closed_spectrum(filter_gains, decay_rates, freq_ids, inner_len, full_len, seq_len)
    product_spec = complex_times(filter_spec, signal_spec)
    product_back = back_section(product_spec, inner_back_half, back_cos, back_sin)
    product_cols = lax.all_to_all(product_back, "context", split_axis=2, concat_axis=1, tiled=True)
    product_part = last_section(product_cols, end_half, 1.0 / full_len)
    conv_out = lax.all_to_all(
        product_part, "context", split_axis=0, concat_axis=1, tiled=True
    ).reshape(row_count, chan_count)
    full_weight = lax.all_gather(out_weight, "context", axis=1, tiled=True)
    gate_grad = lax.dot_general(
        gathered_out, full_weight, (((1,), (1,)), ((), ())), preferred_element_type=jnp.float32
    )
    conv_real = conv_out.astype(jnp.float32)
    query_real = query_proj.astype(jnp.float32)
    gated_out = (query_real * conv_real).astype(jnp.bfloat16)
    grad_query = (gate_grad * conv_real).astype(jnp.bfloat16)
    conv_grad = (gate_grad * query_real).astype(jnp.bfloat16)
    weight_rows = lax.psum_scatter(
        lax.dot_general(
            gathered_out, gated_out, (((0,), (0,)), ((), ())), preferred_element_type=jnp.float32
        ).astype(jnp.bfloat16),
        "context",
        scatter_dimension=0,
        tiled=True,
    ).astype(jnp.float32)
    grad_weight = jnp.transpose(weight_rows) * norm_scale
    grad_spec = forward_signal(conv_grad)
    input_spec = conj_times(filter_spec, grad_spec)
    kernel_spec = conj_times(signal_spec, grad_spec)
    input_back = back_section(input_spec, inner_back_half, back_cos, back_sin)
    kernel_back = back_section(kernel_spec, inner_back_half, back_cos, back_sin)
    input_cols, kernel_cols = (
        lax.all_to_all(input_back, "context", split_axis=2, concat_axis=1, tiled=True),
        lax.all_to_all(kernel_back, "context", split_axis=2, concat_axis=1, tiled=True),
    )
    input_part = last_section(input_cols, end_half, 1.0 / full_len)
    kernel_part = last_section(kernel_cols, end_half, 1.0 / full_len)
    input_moved, kernel_moved = (
        lax.all_to_all(input_part, "context", split_axis=0, concat_axis=1, tiled=True),
        lax.all_to_all(kernel_part, "context", split_axis=0, concat_axis=1, tiled=True),
    )
    input_grad = input_moved.reshape(row_count, chan_count)
    kernel_rows = kernel_moved.reshape(row_count, chan_count)
    gain_part, rate_part = filter_terms(kernel_rows, time_ids, decay_rates, filter_gains)
    grad_gains, grad_rates = (
        lax.psum((gain_part * norm_scale).astype(jnp.bfloat16), "context").astype(jnp.float32),
        lax.psum((rate_part * norm_scale).astype(jnp.bfloat16), "context").astype(jnp.float32),
    )
    input_real = input_grad.astype(jnp.float32)
    grad_key = (input_real * value_proj.astype(jnp.float32)).astype(jnp.bfloat16)
    grad_value = (input_real * key_proj.astype(jnp.float32)).astype(jnp.bfloat16)
    return (grad_query, grad_key, grad_value, grad_gains, grad_rates, grad_weight)


def solution(mesh):
    in_specs = (
        P("context", "tensor"),
        P("context", "tensor"),
        P("context", "tensor"),
        P("tensor", None),
        P("tensor", None),
        P("tensor", "context"),
        P("context", "tensor"),
    )
    out_specs = (
        P("context", "tensor"),
        P("context", "tensor"),
        P("context", "tensor"),
        P("tensor", None),
        P("tensor", None),
        P("tensor", "context"),
    )
    return jax.shard_map(
        on_device, mesh=mesh, in_specs=in_specs, out_specs=out_specs, check_vma=False
    )
```

profile of v0, /device:TPU:64, one launch (start us, length us, event | category | flops | bytes accessed | tf_op | source)
XLA Modules:
  0.0 690.3 jit_solution(7535090144302376511)
XLA Ops:
  8.7 1.3 fusion.54
  10.0 1.1 copy.141
  11.1 8.7 %all-to-all-start = ((bf16[16,32,512]{2,0,1:T(8,128)(2,1)}), bf16[16,32,512]{2,0,1:T(8,128)(2,1)S(1)}, u32[]{:S(2)}, u32[]{:S(2)}) async-start(bf16[16,32,512]{2,0,1:T(8,128)(2,1)} %copy.141), calls=%async_computation | async-start | bytes 1048576 | tf_op jit(solution)/shard_map/all_to_all | solution.py:168
  19.8 45.5 %all-gather.3.cloned.1.call-done = bf16[512,4096]{1,0:T(8,128)(2,1)} async-done(((bf16[512,512]{1,0:T(8,128)(2,1)}), bf16[512,4096]{1,0:T(8,128)(2,1)}) %all-gather.3.cloned.1.call-update) | async-done | bytes 4194320 | tf_op jit(solution)/shard_map/all_gather | solution.py:155
  65.2 160.0 %all-gather.5.cloned.1.call-done = bf16[512,4096]{1,0:T(8,128)(2,1)} async-done(((bf16[512,128]{1,0:T(8,128)(2,1)}), bf16[512,4096]{1,0:T(8,128)(2,1)}) %all-gather.5.cloned.1.call-update) | async-done | bytes 4194320 | tf_op jit(solution)/shard_map/all_gather | solution.py:182
  225.3 6.8 fusion.56
  232.1 1.1 copy.149
  233.2 6.7 all-to-all-start.4
  239.9 8.5 %negate_convert_fusion = (bf16[1024,512]{1,0:T(8,128)(2,1)S(1)}, bf16[1024,512]{1,0:T(8,128)(2,1)S(1)}) fusion(), kind=kLoop, calls=%fused_computation.83 | loop fusion | flops 8912896 | bytes 2097152 | tf_op jit(solution)/shard_map/convert.46
  248.5 3.3 fusion.46
  251.8 1.3 fusion.45
  253.0 0.9 copy-done.7
  253.9 2.3 fusion.60
  256.4 3.6 copy.142
  260.0 8.6 %all-to-all-start.1 = ((bf16[2,1024,1,512]{3,0,2,1:T(2,128)(2,1)}), bf16[2,1024,1,512]{3,0,2,1:T(2,128)(2,1)S(1)}, u32[]{:S(2)}, u32[]{:S(2)}) async-start(bf16[2,1024,1,512]{3,0,2,1:T(2,128)(2,1)} %copy.142), calls=%async_computation.1 | async-start | bytes 4194304 | tf_op jit(solution)/shard_map/all_to_all | solution.py:170
  269.4 1.7 pad_maximum_fusion.4
  271.1 3.5 copy.150
  274.7 22.3 %all-to-all-done.1 = bf16[2,1024,1,512]{3,0,2,1:T(2,128)(2,1)S(1)} async-done(((bf16[2,1024,1,512]{3,0,2,1:T(2,128)(2,1)}), bf16[2,1024,1,512]{3,0,2,1:T(2,128)(2,1)S(1)}, u32[]{:S(2)}, u32[]{:S(2)}) %all-to-all-start.1) | async-done | bytes 2097184 | tf_op jit(solution)/shard_map/all_to_all | solution.py:170
  297.0 1.3 copy-done
  298.3 4.8 all-to-all-start.5
  303.1 23.7 %fusion.2 = (f32[32,32,512]{2,1,0:T(8,128)}, f32[32,32,512]{2,1,0:T(8,128)}) fusion(f32[32,32]{1,0:T(8,128)S(1)} %get-tuple-element.55, f32[512,16]{0,1:T(8,128)S(1)} %get-tuple-element.43, f32[32,32]{1,0:T(8,128)S(1)} %get-tuple-element.54, f32[512,16]{0,1:T(8,128)S(1)} %get-tuple-element.44, f32[512,16]{0,1:T(8,128)S(1)} %get-tuple-element.42, ...), kind=kLoop, calls=%fused_computation.4 | loop fusion | flops 99614720 | bytes 5349376 | tf_op jit(solution)/shard_map/reduce_sum | solution.py:116
  326.8 1.7 fusion.39
  328.6 3.5 fusion.42
  332.1 2.1 fusion.16
  334.1 0.8 convolution_bitcast_fusion.2
  335.0 0.8 convolution_bitcast_fusion.1
  335.8 0.8 convolution_bitcast_fusion
  336.6 4.1 subtract_convert_fusion
  340.9 3.5 copy.145
  344.4 8.2 %all-to-all-start.2 = ((bf16[2,32,32,512]{3,0,1,2:T(2,128)(2,1)}), bf16[2,32,32,512]{3,0,1,2:T(2,128)(2,1)S(1)}, u32[]{:S(2)}, u32[]{:S(2)}) async-start(bf16[2,32,32,512]{3,0,1,2:T(2,128)(2,1)} %copy.145), calls=%async_computation.2 | async-start | bytes 4194304 | tf_op jit(solution)/shard_map/all_to_all | solution.py:177
  352.7 9.2 %negate_convert_fusion.1 = (bf16[512,1024]{1,0:T(8,128)(2,1)}, bf16[512,1024]{1,0:T(8,128)(2,1)}) fusion(), kind=kLoop, calls=%fused_computation.87 | loop fusion | flops 8912896 | bytes 2097152 | tf_op jit(solution)/shard_map/convert.48
  361.9 15.3 %all-to-all-done.2 = bf16[2,32,32,512]{3,0,1,2:T(2,128)(2,1)S(1)} async-done(((bf16[2,32,32,512]{3,0,1,2:T(2,128)(2,1)}), bf16[2,32,32,512]{3,0,1,2:T(2,128)(2,1)S(1)}, u32[]{:S(2)}, u32[]{:S(2)}) %all-to-all-start.2) | async-done | bytes 2097184 | tf_op jit(solution)/shard_map/all_to_all | solution.py:177
  377.7 0.8 copy-done.11
  378.7 2.0 fusion.52
  381.3 2.8 reduce
  384.1 2.2 reshape.520
  386.4 4.6 all-to-all-start.3
  391.2 3.5 copy.157
  394.8 8.5 %all-to-all-done.3 = bf16[32,2,4096]{2,1,0:T(2,128)(2,1)} async-done(((bf16[32,2,4096]{2,1,0:T(2,128)(2,1)}), bf16[32,2,4096]{2,1,0:T(2,128)(2,1)}, u32[]{:S(2)}, u32[]{:S(2)}) %all-to-all-start.3) | async-done | bytes 524320 | tf_op jit(solution)/shard_map/all_to_all | solution.py:179
  403.2 4.0 all-to-all-start.8
  407.3 4.9 reshape.521
  412.2 2.0 copy.148
  414.2 1.1 fusion.57
  415.3 4.4 fusion.4
  419.7 6.5 copy.176
  426.2 1.4 pad_maximum_fusion.5
  427.6 3.5 copy.153
  431.2 5.8 all-to-all-done.8
  436.9 4.8 all-to-all-start.6
  443.3 1.2 fusion.50
  444.5 1.0 reduce.2
  445.6 1.2 reshape.524
  446.7 38.3 %all-to-all-done.6 = bf16[2,32,32,512]{3,0,1,2:T(2,128)(2,1)} async-done(((bf16[2,32,32,512]{3,0,1,2:T(2,128)(2,1)}), bf16[2,32,32,512]{3,0,1,2:T(2,128)(2,1)}, u32[]{:S(2)}, u32[]{:S(2)}) %all-to-all-start.6) | async-done | bytes 2097184 | tf_op jit(solution)/shard_map/all_to_all | solution.py:206
  485.0 7.7 %all-to-all-start.9 = ((bf16[32,2,4096]{2,1,0:T(2,128)(2,1)}), bf16[32,2,4096]{2,1,0:T(2,128)(2,1)S(1)}, u32[]{:S(2)}, u32[]{:S(2)}) async-start(bf16[32,2,4096]{2,1,0:T(2,128)(2,1)} %reshape.524), calls=%async_computation.9 | async-start | bytes 1048576 | tf_op jit(solution)/shard_map/all_to_all | solution.py:213
  492.8 2.1 copy.154
  494.9 1.3 fusion.51
  496.2 1.0 reduce.1
  497.2 1.2 reshape.522
  498.4 8.9 %all-to-all-done.9 = bf16[32,2,4096]{2,1,0:T(2,128)(2,1)S(1)} async-done(((bf16[32,2,4096]{2,1,0:T(2,128)(2,1)}), bf16[32,2,4096]{2,1,0:T(2,128)(2,1)S(1)}, u32[]{:S(2)}, u32[]{:S(2)}) %all-to-all-start.9) | async-done | bytes 524320 | tf_op jit(solution)/shard_map/all_to_all | solution.py:213
  507.3 4.1 all-to-all-start.7
  512.8 6.0 multiply_reduce_fusion.1
  518.9 159.3 %all-reduce = (bf16[512,16]{0,1:T(8,128)(2,1)S(1)}, bf16[512,16]{0,1:T(8,128)(2,1)S(1)}) all-reduce(bf16[512,16]{0,1:T(8,128)(2,1)S(1)} %multiply_convert_fusion.1, bf16[512,16]{0,1:T(8,128)(2,1)S(1)} %multiply_convert_fusion), channel_id=1, replica_groups=mesh['context'=32,'tensor'=8] {'context'}, use_global_device_ids=true, to_apply=%region_3.4 | all-reduce | flops 16384 | bytes 65536 | tf_op jit(solution)/shard_map/psum | solution.py:219
  680.6 1.3 fusion.53
  681.8 1.0 copy.177
  (76 shorter events, 10.3 us)
Async XLA Ops:
  7.2 218.1 %copy-start.16 = (bf16[512,512]{1,0:T(8,128)(2,1)S(1)}, bf16[512,512]{1,0:T(8,128)(2,1)}, u32[]{:S(2)}) copy-start(bf16[512,512]{1,0:T(8,128)(2,1)} %param.7) | copy-start | bytes 1572868
  7.2 58.1 %all-gather.3.cloned.1.call-start = ((), (), s32[]{:S(2)}) async-start(), calls=%async_computation.11 | async-start | bytes 4718592 | tf_op jit(solution)/shard_map/all_gather | solution.py:155
  7.9 217.4 %all-gather.5.cloned.1.call-start = ((), (), s32[]{:S(2)}) async-start(), calls=%async_computation.12 | async-start | bytes 4325376 | tf_op jit(solution)/shard_map/all_gather | solution.py:182
  11.1 222.1 %all-to-all-start = ((bf16[16,32,512]{2,0,1:T(8,128)(2,1)}), bf16[16,32,512]{2,0,1:T(8,128)(2,1)S(1)}, u32[]{:S(2)}, u32[]{:S(2)}) async-start(bf16[16,32,512]{2,0,1:T(8,128)(2,1)} %copy.141), calls=%async_computation | async-start | bytes 1048576 | tf_op jit(solution)/shard_map/all_to_all | solution.py:168
  233.2 18.6 %all-to-all-start.4 = ((bf16[16,32,512]{2,0,1:T(8,128)(2,1)}), bf16[16,32,512]{2,0,1:T(8,128)(2,1)S(1)}, u32[]{:S(2)}, u32[]{:S(2)}) async-start(bf16[16,32,512]{2,0,1:T(8,128)(2,1)} %copy.149), calls=%async_computation.4 | async-start | bytes 1048576 | tf_op jit(solution)/shard_map/all_to_all | solution.py:168
  251.8 2.2 copy-start.7
  260.0 9.2 %copy-start.18 = (f32[512,16]{0,1:T(8,128)S(1)}, f32[512,16]{0,1:T(8,128)}, u32[]{:S(2)}) copy-start(f32[512,16]{0,1:T(8,128)} %param.10) | copy-start | bytes 98308
  260.0 9.2 %copy-start.19 = (f32[512,16]{0,1:T(8,128)S(1)}, f32[512,16]{0,1:T(8,128)}, u32[]{:S(2)}) copy-start(f32[512,16]{0,1:T(8,128)} %param.11) | copy-start | bytes 98308
  260.0 37.0 %all-to-all-start.1 = ((bf16[2,1024,1,512]{3,0,2,1:T(2,128)(2,1)}), bf16[2,1024,1,512]{3,0,2,1:T(2,128)(2,1)S(1)}, u32[]{:S(2)}, u32[]{:S(2)}) async-start(bf16[2,1024,1,512]{3,0,2,1:T(2,128)(2,1)} %copy.142), calls=%async_computation.1 | async-start | bytes 4194304 | tf_op jit(solution)/shard_map/all_to_all | solution.py:170
  297.0 1.3 copy-start
  298.3 30.2 %all-to-all-start.5 = ((bf16[2,1024,1,512]{3,0,2,1:T(2,128)(2,1)}), bf16[2,1024,1,512]{3,0,2,1:T(2,128)(2,1)}, u32[]{:S(2)}, u32[]{:S(2)}) async-start(bf16[2,1024,1,512]{3,0,2,1:T(2,128)(2,1)} %copy.150), calls=%async_computation.5 | async-start | bytes 4194304 | tf_op jit(solution)/shard_map/all_to_all | solution.py:170
  303.1 23.7 %copy-start.1 = (bf16[2,1024,1,512]{3,0,2,1:T(2,128)(2,1)S(1)}, bf16[2,1024,1,512]{3,0,2,1:T(2,128)(2,1)}, u32[]{:S(2)}) copy-start(bf16[2,1024,1,512]{3,0,2,1:T(2,128)(2,1)} %copy-done) | copy-start | bytes 6291460
  328.6 3.5 copy-start.2
  328.6 3.5 copy-start.3
  344.4 32.8 %all-to-all-start.2 = ((bf16[2,32,32,512]{3,0,1,2:T(2,128)(2,1)}), bf16[2,32,32,512]{3,0,1,2:T(2,128)(2,1)S(1)}, u32[]{:S(2)}, u32[]{:S(2)}) async-start(bf16[2,32,32,512]{3,0,1,2:T(2,128)(2,1)} %copy.145), calls=%async_computation.2 | async-start | bytes 4194304 | tf_op jit(solution)/shard_map/all_to_all | solution.py:177
  377.2 1.2 copy-start.11
  377.2 1.5 copy-start.13
  380.8 10.2 %copy-start.5 = (bf16[1,32,32,512]{3,2,0,1:T(8,128)(2,1)S(1)}, bf16[1,32,32,512]{3,2,0,1:T(8,128)(2,1)}, u32[]{:S(2)}) copy-start(bf16[1,32,32,512]{3,2,0,1:T(8,128)(2,1)} %get-tuple-element.16) | copy-start | bytes 3145732
  380.8 10.2 %copy-start.6 = (bf16[1,32,32,512]{3,2,0,1:T(8,128)(2,1)S(1)}, bf16[1,32,32,512]{3,2,0,1:T(8,128)(2,1)}, u32[]{:S(2)}) copy-start(bf16[1,32,32,512]{3,2,0,1:T(8,128)(2,1)} %get-tuple-element.17) | copy-start | bytes 3145732
  386.4 16.9 %all-to-all-start.3 = ((bf16[32,2,4096]{2,1,0:T(2,128)(2,1)}), bf16[32,2,4096]{2,1,0:T(2,128)(2,1)}, u32[]{:S(2)}, u32[]{:S(2)}) async-start(bf16[32,2,4096]{2,1,0:T(2,128)(2,1)} %reshape.520), calls=%async_computation.3 | async-start | bytes 1048576 | tf_op jit(solution)/shard_map/all_to_all | solution.py:179
  403.2 33.7 %all-to-all-start.8 = ((bf16[2,32,32,512]{3,0,1,2:T(2,128)(2,1)}), bf16[2,32,32,512]{3,0,1,2:T(2,128)(2,1)S(1)}, u32[]{:S(2)}, u32[]{:S(2)}) async-start(bf16[2,32,32,512]{3,0,1,2:T(2,128)(2,1)} %copy.157), calls=%async_computation.8 | async-start | bytes 4194304 | tf_op jit(solution)/shard_map/all_to_all | solution.py:207
  407.2 274.6 %reduce-scatter.4.cloned.1.call-start = ((), (), s32[]{:S(2)}) async-start(), calls=%async_computation.13 | async-start | bytes 4325376
  412.2 2.0 copy-start.10
  412.2 2.0 copy-start.17
  412.2 3.1 copy-start.4
  436.9 48.1 %all-to-all-start.6 = ((bf16[2,32,32,512]{3,0,1,2:T(2,128)(2,1)}), bf16[2,32,32,512]{3,0,1,2:T(2,128)(2,1)}, u32[]{:S(2)}, u32[]{:S(2)}) async-start(bf16[2,32,32,512]{3,0,1,2:T(2,128)(2,1)} %copy.153), calls=%async_computation.6 | async-start | bytes 4194304 | tf_op jit(solution)/shard_map/all_to_all | solution.py:206
  441.7 1.2 copy-start.12
  441.7 1.5 copy-start.14
  485.0 22.3 %all-to-all-start.9 = ((bf16[32,2,4096]{2,1,0:T(2,128)(2,1)}), bf16[32,2,4096]{2,1,0:T(2,128)(2,1)S(1)}, u32[]{:S(2)}, u32[]{:S(2)}) async-start(bf16[32,2,4096]{2,1,0:T(2,128)(2,1)} %reshape.524), calls=%async_computation.9 | async-start | bytes 1048576 | tf_op jit(solution)/shard_map/all_to_all | solution.py:213
  492.7 2.2 copy-start.15
  507.3 172.1 %all-to-all-start.7 = ((bf16[32,2,4096]{2,1,0:T(2,128)(2,1)}), bf16[32,2,4096]{2,1,0:T(2,128)(2,1)S(1)}, u32[]{:S(2)}, u32[]{:S(2)}) async-start(bf16[32,2,4096]{2,1,0:T(2,128)(2,1)} %reshape.522), calls=%async_computation.7 | async-start | bytes 1048576 | tf_op jit(solution)/shard_map/all_to_all | solution.py:212
  518.8 161.8 %copy-start.8 = (bf16[512,512]{1,0:T(8,128)(2,1)S(1)}, bf16[512,512]{1,0:T(8,128)(2,1)}, u32[]{:S(2)}) copy-start(bf16[512,512]{1,0:T(8,128)(2,1)} %param.9) | copy-start | bytes 1572868
  518.8 161.8 %copy-start.9 = (bf16[512,512]{1,0:T(8,128)(2,1)S(1)}, bf16[512,512]{1,0:T(8,128)(2,1)}, u32[]{:S(2)}) copy-start(bf16[512,512]{1,0:T(8,128)(2,1)} %param.8) | copy-start | bytes 1572868
Sparse Core Ops, SparseCore 0:
  9.8 55.3 all-gather.2
  67.0 158.2 all-gather.4
  426.3 183.5 reduce-scatter.3
where the time goes:
time: 699 us; the launch traced here: 690 us
  waiting for transfers between devices  306 us (44%)
  blocking collectives  159 us (23%)
  other arithmetic  71.2 us (10%)
  starting transfers between devices  62.2 us (9%)
  local copies, waits for them, and re-layouts  49.2 us (7%)
  matrix products  28 us (4%)
  between operations  14.5 us (2%)
    all_gather x1, waiting for transfers between devices, on_device(): full_weight = lax.all_gather(out_weight, 'context', axis=1, tiled=True)  160 us
    psum x1, blocking collectives, on_device(): lax.psum((gain_part * norm_scale).astype(jnp.bfloat16), 'context')  159 us
    all_gather x1, waiting for transfers between devices, on_device(): gathered_out = lax.all_gather(grad_out, 'tensor', axis=1, tiled=True)  45.5 us
    all_to_all x1, waiting for transfers between devices, on_device(): lax.all_to_all(input_back, 'context', split_axis=2, concat_axis=1, tiled=...  38.3 us
    another operation x7, other arithmetic  24.2 us
    reduce_sum x1, other arithmetic, closed_spectrum(): imag_acc = -jnp.sum(numer_scale * den_imag, axis=3)  23.7 us
    unnamed x48, local copies, waits for them, and re-layouts  22.4 us
    all_to_all x2, waiting for transfers between devices, forward_signal(): lax.all_to_all(turned, 'context', split_axis=1, concat_axis=2, tiled=True)  22.3 us
  transfers between devices with their start and end apart: 13, of which 8 were waited for; matrix products, arithmetic and copies ran while one was open for 16% of the time, Pallas kernels for 0%

commit v1 on v0

v1 whole, which is shorter than its diff:
```python
import math

import jax
import jax.numpy as jnp
from jax import lax
from jax.experimental import pallas as pl
from jax.experimental.pallas import tpu as pltpu
from jax.sharding import PartitionSpec as P

BF16 = jnp.bfloat16
F32 = jnp.float32
MESH = pl.DeviceIdType.MESH

NCTX = 32
ROWS = 512
CH = 512
MODES = 16
SUB = 8
STEPS = ROWS // SUB
LANES = 128
GROUPS = CH // LANES
SEQ = ROWS * NCTX
NORM = 1.0 / math.sqrt(SEQ)

N_A = 11
N_W = 17
N_O = 25
OFF_W = N_A
OFF_O = OFF_W + N_W
N_RING = OFF_O + N_O


def shift_sub(val, step):
    rolled = pltpu.roll(val, step % SUB, 1)
    ids = lax.broadcasted_iota(jnp.int32, val.shape, 1)
    keep = ids >= step if step > 0 else ids < SUB + step
    return jnp.where(keep, rolled, 0.0)


def kernel(
    q_ref, k_ref, v_ref, gain2, rate2, gain3, rate3, w_ref, go_ref,
    gq_out, gk_out, gv_out, yz_out, ow_out,
    ag, wg, op, xs, gs, ys, perm, perm_t, a8, amp8, ebuf, eall, qbuf, qall, hd3, st2,
    scr8, hfwd, hbwd, tend, gate, cv, gt, yz, yz_in, yz_all,
    opp_y0, fin_y0, opp_x0, fin_x0, opp_x1, fin_x1, opp_y1, fin_y1,
    v0, v1, rsum, rsend, zin,
    ring_s, ring_r, e_s, e_r, q_s, q_r, y_s, y_r, o_s, o_r, loc,
):
    c = lax.axis_index("context")
    t = lax.axis_index("tensor")
    x = c // 8
    y = (c // 2) % 4
    zl = c % 2
    zh = t // 2
    core = t % 2

    def ctx_of(xx, yy, zz):
        return xx * 8 + yy * 2 + zz

    x_right = ctx_of((x + 1) % 4, y, zl)
    x_left = ctx_of((x + 3) % 4, y, zl)
    y_right = ctx_of(x, (y + 1) % 4, zl)
    y_left = ctx_of(x, (y + 3) % 4, zl)
    z_peer = ctx_of(x, y, 1 - zl)
    partner = zh * 2 + (1 - core)
    t_right = ((zh + 1) % 4) * 2 + core
    t_left = ((zh + 3) % 4) * 2 + core
    t_opp = ((zh + 2) % 4) * 2 + core

    pending = []

    def remote(index, src, dst, ctx, ten):
        copy = pltpu.make_async_remote_copy(
            src_ref=src, dst_ref=dst, send_sem=ring_s.at[index], recv_sem=ring_r.at[index],
            device_id=(ctx, ten), device_id_type=MESH,
        )
        copy.start()
        pending.append(copy)
        return copy

    barrier = pltpu.get_barrier_semaphore()

    def greet(d, _):
        pl.semaphore_signal(barrier, inc=1, device_id=((c + d) % NCTX, t), device_id_type=MESH)
        return 0

    lax.fori_loop(1, NCTX, greet, 0)
    for ten in (partner, t_right, t_left):
        pl.semaphore_signal(barrier, inc=1, device_id=(c, ten), device_id_type=MESH)
    pl.semaphore_wait(barrier, NCTX - 1 + 3)

    lo, hi = pl.ds(0, 256), pl.ds(256, 256)
    wz = remote(
        OFF_W, w_ref, wg.at[x, y, :, pl.ds(pl.multiple_of(zl * 128, 128), 128)], z_peer, t
    )
    a_r0 = remote(0, go_ref.at[lo], ag.at[t, lo], c, t_right)
    a_l1 = remote(1, go_ref.at[hi], ag.at[t, hi], c, t_left)
    a_r1 = remote(2, go_ref.at[hi], ag.at[t, hi], c, t_right)
    a_l0 = remote(3, go_ref.at[lo], ag.at[t, lo], c, t_left)
    a_p = remote(4, go_ref, ag.at[t], c, partner)
    own_a = pltpu.make_async_copy(go_ref, ag.at[t], loc.at[0])
    own_w = pltpu.make_async_copy(
        w_ref, wg.at[x, y, :, pl.ds(pl.multiple_of(zl * 128, 128), 128)], loc.at[1]
    )
    own_a.start()
    own_w.start()

    rate_wide = jnp.exp(rate3[...])
    a8[...] = jnp.broadcast_to(jnp.exp(-rate_wide), a8.shape)
    amp8[...] = jnp.broadcast_to(gain3[...] * jnp.sqrt(2.0 * rate_wide), amp8.shape)
    row_id = lax.broadcasted_iota(jnp.int32, (ROWS, ROWS), 0)
    col_id = lax.broadcasted_iota(jnp.int32, (ROWS, ROWS), 1)
    perm[...] = jnp.where(col_id == STEPS * (row_id % SUB) + row_id // SUB, 1.0, 0.0).astype(BF16)
    perm_t[...] = jnp.where(row_id == STEPS * (col_id % SUB) + col_id // SUB, 1.0, 0.0).astype(BF16)

    def spread(dst, natural):
        mixed = jnp.dot(perm[...], natural, preferred_element_type=F32)
        for grp in range(GROUPS):
            dst[grp] = mixed[:, grp * LANES:(grp + 1) * LANES]

    def gather_back():
        mixed = jnp.concatenate([ys[grp] for grp in range(GROUPS)], axis=1).astype(BF16)
        return jnp.dot(perm_t[...], mixed, preferred_element_type=F32)

    signal = (k_ref[...].astype(F32) * v_ref[...].astype(F32)).astype(BF16)
    spread(xs, signal)

    def lane_at(grp):
        return pl.ds(pl.multiple_of(grp * LANES, LANES), LANES)

    def step_rows(j):
        return pl.ds(pl.multiple_of(j * SUB, SUB), SUB)

    def rates_at(grp):
        return jnp.exp(rate3[:, :, lane_at(grp)])

    UNROLL = 4

    def end_states(src, backward, hsub):
        def group(grp, _):
            decay = a8[:, :, lane_at(grp)]

            def step(i, state):
                for u in range(UNROLL):
                    j = i * UNROLL + u
                    j = STEPS - 1 - j if backward else j
                    state = decay * state + src[grp, step_rows(j)][None]
                return state

            state = lax.fori_loop(
                0, STEPS // UNROLL, step, jnp.zeros((MODES, SUB, LANES), F32)
            )
            rates = rates_at(grp)
            sign = -1 if backward else 1
            for power in (1, 2, 4):
                factor = jnp.exp(-rates * float(STEPS * power))
                state = state + factor * shift_sub(state, sign * power)
            hsub[:, :, lane_at(grp)] = shift_sub(state, sign)
            scr8[grp, 0:MODES] = state
            return 0

        lax.fori_loop(0, GROUPS, group, 0)
        edge = 0 if backward else SUB - 1
        for grp in range(GROUPS):
            for m in range(MODES):
                st2[m:m + 1, grp * LANES:(grp + 1) * LANES] = scr8[grp, m, edge:edge + 1, :]

    def add_incoming(state, backward, hsub):
        for m in range(MODES):
            hd3[m] = state[m:m + 1, :]

        def group(grp, _):
            ids = lax.broadcasted_iota(jnp.int32, (MODES, SUB, LANES), 1).astype(F32)
            ids = (SUB - 1.0) - ids if backward else ids
            weight = jnp.exp(-rates_at(grp) * (ids * float(STEPS)))
            hsub[:, :, lane_at(grp)] += weight * hd3[:, :, lane_at(grp)]
            return 0

        lax.fori_loop(0, GROUPS, group, 0)

    end_states(xs, False, hfwd)
    ebuf[...] = st2[...].astype(BF16)

    def e_copy(d, index):
        other = (c + d) % NCTX
        return pltpu.make_async_remote_copy(
            src_ref=ebuf, dst_ref=eall.at[index], send_sem=e_s.at[other], recv_sem=e_r.at[index],
            device_id=(other, t), device_id_type=MESH,
        )

    def q_copy(d, index):
        other = (c + d) % NCTX
        return pltpu.make_async_remote_copy(
            src_ref=qbuf, dst_ref=qall.at[index], send_sem=q_s.at[other], recv_sem=q_r.at[index],
            device_id=(other, t), device_id_type=MESH,
        )

    def run(first, last, fun):
        def body(i, carry):
            fun(i)
            return carry

        lax.fori_loop(first, last, body, 0)

    run(1, NCTX - c, lambda d: e_copy(d, c).start())

    own_w.wait()
    wz.wait_recv()
    w0, w1 = pl.ds(0, 256), pl.ds(256, 256)
    w0a, w0b, w1a, w1b = pl.ds(0, 128), pl.ds(128, 128), pl.ds(256, 128), pl.ds(384, 128)
    i = OFF_W + 1
    s_xr = remote(i + 0, wg.at[x, y, w0], wg.at[x, y, w0], x_right, t)
    s_xl = remote(i + 1, wg.at[x, y, w0], wg.at[x, y, w0], x_left, t)
    s_yr = remote(i + 2, wg.at[x, y, w1], wg.at[x, y, w1], y_right, t)
    s_yl = remote(i + 3, wg.at[x, y, w1], wg.at[x, y, w1], y_left, t)
    xm, xp, ym, yp = (x + 3) % 4, (x + 1) % 4, (y + 3) % 4, (y + 1) % 4
    s_xr.wait_recv()
    f_xr = remote(i + 4, wg.at[xm, y, w0a], wg.at[xm, y, w0a], x_right, t)
    s_yr.wait_recv()
    f_yr = remote(i + 6, wg.at[x, ym, w1a], wg.at[x, ym, w1a], y_right, t)
    s_xl.wait_recv()
    f_xl = remote(i + 5, wg.at[xp, y, w0b], wg.at[xp, y, w0b], x_left, t)
    s_yl.wait_recv()
    f_yl = remote(i + 7, wg.at[x, yp, w1b], wg.at[x, yp, w1b], y_left, t)
    f_xr.wait_recv()
    f_xl.wait_recv()
    g_yr = remote(i + 8, wg.at[:, y, w0], wg.at[:, y, w0], y_right, t)
    g_yl = remote(i + 9, wg.at[:, y, w0], wg.at[:, y, w0], y_left, t)
    f_yr.wait_recv()
    f_yl.wait_recv()
    g_xr = remote(i + 10, wg.at[x, :, w1], wg.at[x, :, w1], x_right, t)
    g_xl = remote(i + 11, wg.at[x, :, w1], wg.at[x, :, w1], x_left, t)

    run(0, c, lambda j: e_copy(j - c + NCTX, j).wait_recv())
    chunk_decay = jnp.exp(-jnp.exp(rate2[...]) * float(ROWS))
    head = lax.fori_loop(
        0, c, lambda j, h: chunk_decay * h + eall[j].astype(F32), jnp.zeros((MODES, CH), F32)
    )
    add_incoming(head, False, hfwd)

    def scan_out(src, backward, hsub):
        def group(grp, _):
            decay = a8[:, :, lane_at(grp)]
            amp = amp8[:, :, lane_at(grp)]

            def step(i, state):
                for u in range(UNROLL):
                    j = i * UNROLL + u
                    j = STEPS - 1 - j if backward else j
                    state = decay * state + src[grp, step_rows(j)][None]
                    ys[grp, step_rows(j)] = jnp.sum(amp * state, axis=0)
                return state

            lax.fori_loop(0, STEPS // UNROLL, step, hsub[:, :, lane_at(grp)])
            return 0

        lax.fori_loop(0, GROUPS, group, 0)

    scan_out(xs, False, hfwd)
    cv[...] = gather_back().astype(BF16)
    gated = (q_ref[...].astype(F32) * cv[...].astype(F32)).astype(BF16).astype(F32)
    gt[...] = jnp.transpose(gated).astype(BF16)

    tl, tr, to = t_left, t_right, t_opp
    a_r0.wait_recv()
    f_r = remote(5, ag.at[tl, lo], ag.at[tl, lo], c, t_right)
    a_l1.wait_recv()
    f_l = remote(6, ag.at[tr, hi], ag.at[tr, hi], c, t_left)
    a_r1.wait_recv()
    p_l = remote(7, ag.at[tl], ag.at[tl], c, partner)
    a_l0.wait_recv()
    p_r = remote(8, ag.at[tr], ag.at[tr], c, partner)

    g_yr.wait_recv()
    h_yr = remote(i + 12, wg.at[:, ym, w0a], wg.at[:, ym, w0a], y_right, t)
    g_xr.wait_recv()
    h_xr = remote(i + 14, wg.at[xm, :, w1a], wg.at[xm, :, w1a], x_right, t)
    g_yl.wait_recv()
    h_yl = remote(i + 13, wg.at[:, yp, w0b], wg.at[:, yp, w0b], y_left, t)
    g_xl.wait_recv()
    h_xl = remote(i + 15, wg.at[xp, :, w1b], wg.at[xp, :, w1b], x_left, t)

    f_r.wait_recv()
    p_a = remote(9, ag.at[to, lo], ag.at[to, lo], c, partner)
    f_l.wait_recv()
    p_b = remote(10, ag.at[to, hi], ag.at[to, hi], c, partner)
    own_a.wait()
    a_p.wait_recv()
    p_l.wait_recv()
    p_r.wait_recv()
    p_a.wait_recv()
    p_b.wait_recv()

    def out_block(j):
        half = pl.ds(pl.multiple_of((j % 2) * 256, 256), 256)
        op[j // 4, j % 4] = jnp.dot(
            gt[...], ag[j // 2, :, half], preferred_element_type=F32
        ).astype(BF16)

    run(0, 16, out_block)

    def send_ring(base, unit, opp, fin, pos, right, left):
        far, nxt, prv = (pos + 2) % 4, (pos + 1) % 4, (pos + 3) % 4
        o_r_ = remote(base + 0, unit(far, 0), opp.at[0], right, t)
        o_l_ = remote(base + 1, unit(far, 1), opp.at[1], left, t)
        d_r = remote(base + 2, unit(nxt, 1), fin.at[0, 1], right, t)
        d_l = remote(base + 3, unit(prv, 0), fin.at[1, 0], left, t)
        return (base, unit, opp, fin, nxt, prv, right, left, o_r_, o_l_, d_r, d_l)

    def add_ring(ring):
        base, unit, opp, fin, nxt, prv, right, left, o_r_, o_l_, d_r, d_l = ring
        o_r_.wait_recv()
        ref = unit(nxt, 0)
        ref[...] = (ref[...].astype(F32) + opp[0].astype(F32)).astype(BF16)
        e_r_ = remote(base + 4, ref, fin.at[0, 0], right, t)
        o_l_.wait_recv()
        ref = unit(prv, 1)
        ref[...] = (ref[...].astype(F32) + opp[1].astype(F32)).astype(BF16)
        e_l_ = remote(base + 5, ref, fin.at[1, 1], left, t)
        return (d_r, d_l, e_r_, e_l_)

    def ring_sum(unit, fin, pos, waits, part):
        return (
            unit(pos, part)[...].astype(F32) + fin[0, part].astype(F32) + fin[1, part].astype(F32)
        )

    def unit_y0(target, part):
        return op.at[:, target, pl.ds(part * 128, 128)]

    def unit_x1(target, part):
        return op.at[target, :, pl.ds(256 + part * 128, 128)]

    def unit_x0(target, part):
        return v0.at[target, pl.ds(part * 128, 128)]

    def unit_y1(target, part):
        return v1.at[target, pl.ds(part * 128, 128)]

    ring_a = send_ring(OFF_O, unit_y0, opp_y0, fin_y0, y, y_right, y_left)
    ring_b = send_ring(OFF_O + 6, unit_x1, opp_x1, fin_x1, x, x_right, x_left)

    h_yr.wait_recv()
    h_yl.wait_recv()
    h_xr.wait_recv()
    h_xl.wait_recv()
    gate[...] = jnp.zeros_like(gate)
    dims = (((1,), (1,)), ((), ()))

    def gate_block(j):
        rows = ag.at[j]
        gate[...] += lax.dot_general(
            rows[:, 0:256], wg[j // 2, (j % 2) * 2], dims, preferred_element_type=F32
        ) + lax.dot_general(
            rows[:, 256:512], wg[j // 2, (j % 2) * 2 + 1], dims, preferred_element_type=F32
        )

    run(0, 8, gate_block)
    gq_out[...] = (gate[...] * cv[...].astype(F32)).astype(BF16)
    conv_grad = (gate[...] * q_ref[...].astype(F32)).astype(BF16)
    spread(gs, conv_grad)

    def gain_scan(grp, _):
        for part in range(2):
            mode = pl.ds(part * 8, 8)
            decay = a8[mode, :, lane_at(grp)]

            def step(i, carry):
                state, timed, gain_sum, rate_sum = carry
                for u in range(UNROLL):
                    rows = step_rows(i * UNROLL + u)
                    grad = gs[grp, rows][None]
                    decayed = decay * state
                    timed = decay * timed + decayed
                    state = decayed + xs[grp, rows][None]
                    gain_sum = gain_sum + grad * state
                    rate_sum = rate_sum + grad * timed
                return (state, timed, gain_sum, rate_sum)

            zero = jnp.zeros((8, SUB, LANES), F32)
            _, timed, gain_sum, rate_sum = lax.fori_loop(
                0, STEPS // UNROLL, step, (hfwd[mode, :, lane_at(grp)], zero, zero, zero)
            )
            tend[mode, :, lane_at(grp)] = timed
            scr8[grp, mode] = gain_sum
            scr8[grp, pl.ds(MODES + part * 8, 8)] = rate_sum
        return 0

    end_states(gs, True, hbwd)
    qbuf[...] = st2[...].astype(BF16)
    run(NCTX - c, NCTX, lambda d: q_copy(d, c).start())

    waits_a = add_ring(ring_a)
    waits_b = add_ring(ring_b)
    lax.fori_loop(0, GROUPS, gain_scan, 0)
    for grp in range(GROUPS):
        yz[0:MODES, grp] = jnp.sum(scr8[grp, 0:MODES], axis=1)
        yz[MODES:2 * MODES, grp] = jnp.sum(scr8[grp, MODES:2 * MODES], axis=1)

    for copy in waits_a:
        copy.wait_recv()
    for part in range(2):
        total = ring_sum(unit_y0, fin_y0, y, None, part)
        v0[:, part * 128:(part + 1) * 128] = total.astype(BF16)
    ring_c = send_ring(OFF_O + 12, unit_x0, opp_x0, fin_x0, x, x_right, x_left)
    for copy in waits_b:
        copy.wait_recv()
    for part in range(2):
        total = ring_sum(unit_x1, fin_x1, x, None, part)
        v1[:, part * 128:(part + 1) * 128] = total.astype(BF16)
    ring_d = send_ring(OFF_O + 18, unit_y1, opp_y1, fin_y1, y, y_right, y_left)

    run(c + 1, NCTX, lambda j: q_copy(j - c, j).wait_recv())
    tail = lax.fori_loop(
        0, NCTX - 1 - c,
        lambda j, h: chunk_decay * h + qall[NCTX - 1 - j].astype(F32),
        jnp.zeros((MODES, CH), F32),
    )
    add_incoming(tail, True, hbwd)
    for grp in range(GROUPS):
        lanes = slice(grp * LANES, (grp + 1) * LANES)
        cross = jnp.sum(tend[:, :, lanes] * a8[:, :, lanes] * hbwd[:, :, lanes], axis=1)
        yz[MODES:2 * MODES, grp] += cross

    def y_copy(d, index):
        other = (c + d) % NCTX
        return pltpu.make_async_remote_copy(
            src_ref=yz.at[other], dst_ref=yz_in.at[index], send_sem=y_s.at[other],
            recv_sem=y_r.at[index], device_id=(other, t), device_id_type=MESH,
        )

    run(1, NCTX, lambda d: y_copy(d, c).start())

    waits_c = add_ring(ring_c)
    waits_d = add_ring(ring_d)

    scan_out(gs, True, hbwd)
    input_grad = gather_back().astype(BF16).astype(F32)
    gk_out[...] = (input_grad * v_ref[...].astype(F32)).astype(BF16)
    gv_out[...] = (input_grad * k_ref[...].astype(F32)).astype(BF16)

    for copy in waits_c:
        copy.wait_recv()
    for part in range(2):
        rsum[part * 128:(part + 1) * 128] = ring_sum(unit_x0, fin_x0, x, None, part)
    for copy in waits_d:
        copy.wait_recv()
    for part in range(2):
        rsum[256 + part * 128:256 + (part + 1) * 128] = ring_sum(unit_y1, fin_y1, y, None, part)
    rsend[...] = rsum[:, pl.ds(pl.multiple_of((1 - zl) * 128, 128), 128)].astype(BF16)
    z_copy = remote(OFF_O + 24, rsend, zin, z_peer, t)

    run(1, NCTX, lambda d: y_copy(d, (c + d) % NCTX).wait_recv())
    yz_in[c] = yz[c]
    yz_all[c] = jnp.sum(yz_in[...], axis=0)

    def o_copy(d, index):
        other = (c + d) % NCTX
        return pltpu.make_async_remote_copy(
            src_ref=yz_all.at[c], dst_ref=yz_all.at[index], send_sem=o_s.at[other],
            recv_sem=o_r.at[index], device_id=(other, t), device_id_type=MESH,
        )

    run(1, NCTX, lambda d: o_copy(d, c).start())

    z_copy.wait_recv()
    ow_out[...] = (
        rsum[:, pl.ds(pl.multiple_of(zl * 128, 128), 128)] + zin[...].astype(F32)
    ) * NORM

    run(1, NCTX, lambda d: o_copy(d, (c + d) % NCTX).wait_recv())
    yz_out[...] = yz_all[...]
    run(1, NCTX - c, lambda d: e_copy(d, c).wait_send())
    run(NCTX - c, NCTX, lambda d: q_copy(d, c).wait_send())
    run(1, NCTX, lambda d: y_copy(d, c).wait_send())
    run(1, NCTX, lambda d: o_copy(d, c).wait_send())
    for copy in pending:
        copy.wait_send()


def on_device(query_proj, key_proj, value_proj, filter_gains, log_rates, out_weight, grad_out):
    gain2 = filter_gains.T
    rate2 = log_rates.T
    vmem = pl.BlockSpec(memory_space=pltpu.VMEM)
    shape = jax.ShapeDtypeStruct
    dma = pltpu.SemaphoreType.DMA
    wide = (MODES, SUB, CH)
    grad_query, grad_key, grad_value, sums, grad_weight = pl.pallas_call(
        kernel,
        out_shape=(
            shape((ROWS, CH), BF16),
            shape((ROWS, CH), BF16),
            shape((ROWS, CH), BF16),
            shape((2 * MODES, GROUPS, LANES), F32),
            shape((CH, 128), F32),
        ),
        in_specs=[vmem] * 9,
        out_specs=[vmem] * 5,
        scratch_shapes=[
            pltpu.VMEM((8, ROWS, 512), BF16),
            pltpu.VMEM((4, 4, CH, 256), BF16),
            pltpu.VMEM((4, 4, CH, 256), BF16),
            pltpu.VMEM((GROUPS, ROWS, LANES), F32),
            pltpu.VMEM((GROUPS, ROWS, LANES), F32),
            pltpu.VMEM((GROUPS, ROWS, LANES), F32),
            pltpu.VMEM((ROWS, ROWS), BF16),
            pltpu.VMEM((ROWS, ROWS), BF16),
            pltpu.VMEM(wide, F32),
            pltpu.VMEM(wide, F32),
            pltpu.VMEM((MODES, CH), BF16),
            pltpu.VMEM((NCTX, MODES, CH), BF16),
            pltpu.VMEM((MODES, CH), BF16),
            pltpu.VMEM((NCTX, MODES, CH), BF16),
            pltpu.VMEM((MODES, 1, CH), F32),
            pltpu.VMEM((MODES, CH), F32),
            pltpu.VMEM((GROUPS, 2 * MODES, SUB, LANES), F32),
            pltpu.VMEM(wide, F32),
            pltpu.VMEM(wide, F32),
            pltpu.VMEM(wide, F32),
            pltpu.VMEM((ROWS, CH), F32),
            pltpu.VMEM((ROWS, CH), BF16),
            pltpu.VMEM((CH, ROWS), BF16),
            pltpu.VMEM((2 * MODES, GROUPS, LANES), F32),
            pltpu.VMEM((NCTX, GROUPS, LANES), F32),
            pltpu.VMEM((NCTX, GROUPS, LANES), F32),
            pltpu.VMEM((2, 4, 128, 256), BF16),
            pltpu.VMEM((2, 2, 4, 128, 256), BF16),
            pltpu.VMEM((2, 128, 256), BF16),
            pltpu.VMEM((2, 2, 128, 256), BF16),
            pltpu.VMEM((2, 4, 128, 256), BF16),
            pltpu.VMEM((2, 2, 4, 128, 256), BF16),
            pltpu.VMEM((2, 128, 256), BF16),
            pltpu.VMEM((2, 2, 128, 256), BF16),
            pltpu.VMEM((4, 256, 256), BF16),
            pltpu.VMEM((4, 256, 256), BF16),
            pltpu.VMEM((CH, 256), F32),
            pltpu.VMEM((CH, 128), BF16),
            pltpu.VMEM((CH, 128), BF16),
            dma((N_RING,)),
            dma((N_RING,)),
            dma((NCTX,)),
            dma((NCTX,)),
            dma((NCTX,)),
            dma((NCTX,)),
            dma((NCTX,)),
            dma((NCTX,)),
            dma((NCTX,)),
            dma((NCTX,)),
            dma((2,)),
        ],
        compiler_params=pltpu.CompilerParams(
            collective_id=0, has_side_effects=True, vmem_limit_bytes=56 * 1024 * 1024
        ),
        cost_estimate=pl.CostEstimate(
            flops=5_000_000_000, bytes_accessed=5_000_000, transcendentals=0
        ),
    )(
        query_proj, key_proj, value_proj, gain2, rate2,
        gain2[:, None, :], rate2[:, None, :], out_weight, grad_out,
    )
    flat = sums.reshape(2 * MODES, CH).T
    gain_sum, rate_sum = flat[:, :MODES], flat[:, MODES:]
    rates = jnp.exp(log_rates)
    scale = NORM * jnp.sqrt(2.0 * rates)
    grad_gains = scale * gain_sum
    grad_rates = scale * filter_gains * (0.5 * gain_sum - rates * rate_sum)
    return (grad_query, grad_key, grad_value, grad_gains, grad_rates, grad_weight)


def solution(mesh):
    in_specs = (
        P("context", "tensor"),
        P("context", "tensor"),
        P("context", "tensor"),
        P("tensor", None),
        P("tensor", None),
        P("tensor", "context"),
        P("context", "tensor"),
    )
    out_specs = (
        P("context", "tensor"),
        P("context", "tensor"),
        P("context", "tensor"),
        P("tensor", None),
        P("tensor", None),
        P("tensor", "context"),
    )
    return jax.shard_map(
        on_device, mesh=mesh, in_specs=in_specs, out_specs=out_specs, check_vma=False
    )
```

time: 699 us -> 126 us (0.18)
  the two profiles are of different devices: /device:TPU:64 before, /device:TPU:32 now
where the time goes in v1:
time: 126 us
  Pallas kernels  117 us (93%)
  local copies, waits for them, and re-layouts  7.86 us (6%)
    pallas_call x1, Pallas kernels, on_device(): pl.pallas_call(kernel, out_shape=(shape((ROWS, CH), BF16), shape((ROWS, C...  117 us
    unnamed x17, local copies, waits for them, and re-layouts  5.83 us

profile of v1, /device:TPU:32, one launch (start us, length us, event | category | flops | bytes accessed | tf_op | source)
XLA Modules:
  0.0 126.1 jit_solution(3838507699568811940)
XLA Ops:
  0.6 0.0 copy-start.4
  0.6 1.4 %broadcast_in_dim.6.gain3 = f32[16,1,512]{2,1,0:T(1,128)} reshape(f32[16,512]{1,0:T(8,128)} %bitcast.10) | data formatting | bytes 65536 | tf_op jit(solution)/shard_map/broadcast_in_dim | solution.py:558
  2.0 0.0 copy-done.4
  2.0 0.6 broadcast_in_dim.7.rate3
  2.7 116.9 %shard_map.118 = (bf16[512,512]{1,0:T(8,128)(2,1)}, bf16[512,512]{1,0:T(8,128)(2,1)}, bf16[512,512]{1,0:T(8,128)(2,1)}, f32[32,4,128]{2,1,0:T(4,128)}, f32[512,128]{1,0:T(8,128)}) custom-call(bf16[512,512]{1,0:T(8,128)(2,1)} %q_ref.1, bf16[512,512]{1,0:T(8,128)(2,1)} %k_ref.1, bf16[512,512]{1,0:T(8,128)(2,1)} %v_ref.1, f32[16,512]{1,0:T(8,128)} %bitcast.11, ...), custom_call_target="tpu_custom_call" | custom-call | flops 5000000000 | bytes 5000000 | tf_op jit(solution)/shard_map/pallas_call | solution.py:487
  119.6 0.0 copy-start.3
  119.6 0.0 copy-start.5
  119.7 0.9 copy.15
  120.5 0.0 copy-done.3
  120.5 0.0 copy-done.5
  120.5 0.7 fusion.1
  121.2 0.0 copy-start.1
  121.2 1.9 %copy.20 = bf16[512,512]{1,0:T(8,128)(2,1)} copy(bf16[512,512]{1,0:T(8,128)(2,1)} %get-tuple-element.24) | data formatting | bytes 1048576
  123.1 0.0 copy-done.1
  123.1 0.0 copy-start
  123.1 0.8 copy.21
  123.9 0.4 copy-done
  124.3 0.0 copy-start.2
  124.3 0.8 copy.22
  125.1 0.3 copy-done.2
  125.4 0.7 copy.23
Async XLA Ops:
  0.6 1.4 %copy-start.4 = (f32[512,16]{0,1:T(8,128)S(1)}, f32[512,16]{0,1:T(8,128)}, u32[]{:S(2)}) copy-start(f32[512,16]{0,1:T(8,128)} %param.11) | copy-start | bytes 98308
  119.6 0.9 copy-start.3
  119.6 0.9 copy-start.5
  121.2 1.9 %copy-start.1 = (bf16[512,512]{1,0:T(8,128)(2,1)S(1)}, bf16[512,512]{1,0:T(8,128)(2,1)}, u32[]{:S(2)}) copy-start(bf16[512,512]{1,0:T(8,128)(2,1)} %get-tuple-element.25) | copy-start | bytes 1572868
  123.1 1.2 copy-start
  124.3 1.1 copy-start.2

commit v2 on v1

v2 whole, which is shorter than its diff:
```python
import math

import jax
import jax.numpy as jnp
from jax import lax
from jax.experimental import pallas as pl
from jax.experimental.pallas import tpu as pltpu
from jax.sharding import PartitionSpec as P

BF16 = jnp.bfloat16
F32 = jnp.float32
MESH = pl.DeviceIdType.MESH

NCTX = 32
ROWS = 512
CH = 512
MODES = 16
SUB = 8
STEPS = ROWS // SUB
LANES = 128
GROUPS = CH // LANES
SEQ = ROWS * NCTX
NORM = 1.0 / math.sqrt(SEQ)

N_A = 36
N_W = 29
N_O = 6 * 4 + 6 + 6 + 6 + 1
OFF_W = N_A
OFF_O = OFF_W + N_W
N_RING = OFF_O + N_O
PLANE = 16
W_SPLIT = 256


def shift_sub(val, step):
    rolled = pltpu.roll(val, step % SUB, 1)
    ids = lax.broadcasted_iota(jnp.int32, val.shape, 1)
    keep = ids >= step if step > 0 else ids < SUB + step
    return jnp.where(keep, rolled, 0.0)


def kernel(
    q_ref, k_ref, v_ref, gain2, rate2, w_ref, go_ref,
    gq_out, gk_out, gv_out, gain_out, rate_out, ow_out,
    rate3, ag, wg, op, xs, gs, ys, perm, perm_t, a8, amp8,
    ebuf, epeer, esend, eall, qbuf, qpeer, qsend, qall, hd3, st2,
    scr8, hfs, hft, hbwd, gate, cv, gt, yz, yz_in, yz_all,
    oppx, finx, vsum, oppy, finy, oppb, finb, vcol, oppv, finv, rsum, rsend, zin,
    ring_s, ring_r, e_s, e_r, q_s, q_r, y_s, y_r, o_s, o_r, pair_s, pair_r, loc,
):
    c = lax.axis_index("context")
    t = lax.axis_index("tensor")
    x = c // 8
    y = (c // 2) % 4
    zl = c % 2
    zh = t // 2
    core = t % 2
    plane = c // 2

    def ctx_of(xx, yy, zz):
        return xx * 8 + yy * 2 + zz

    xm, xp, xo = (x + 3) % 4, (x + 1) % 4, (x + 2) % 4
    ym, yp, yo = (y + 3) % 4, (y + 1) % 4, (y + 2) % 4
    zm, zp, zo = (zh + 3) % 4, (zh + 1) % 4, (zh + 2) % 4
    x_right, x_left = ctx_of(xp, y, zl), ctx_of(xm, y, zl)
    y_right, y_left = ctx_of(x, yp, zl), ctx_of(x, ym, zl)
    z_peer = ctx_of(x, y, 1 - zl)
    partner = zh * 2 + (1 - core)
    t_right, t_left = zp * 2 + core, zm * 2 + core

    pending = []

    def remote(index, src, dst, ctx, ten):
        copy = pltpu.make_async_remote_copy(
            src_ref=src, dst_ref=dst, send_sem=ring_s.at[index], recv_sem=ring_r.at[index],
            device_id=(ctx, ten), device_id_type=MESH,
        )
        copy.start()
        pending.append(copy)
        return copy

    def run(first, last, fun):
        def body(i, carry):
            fun(i)
            return carry

        lax.fori_loop(first, last, body, 0)

    barrier = pltpu.get_barrier_semaphore()

    def greet(d):
        pl.semaphore_signal(barrier, inc=1, device_id=((c + d) % NCTX, t), device_id_type=MESH)

    run(1, NCTX, greet)
    for ten in (partner, t_right, t_left):
        pl.semaphore_signal(barrier, inc=1, device_id=(c, ten), device_id_type=MESH)
    pl.semaphore_wait(barrier, NCTX - 1 + 3)

    lane_half = [pl.ds(0, 256), pl.ds(256, 256)]
    mine, theirs = pl.multiple_of(core * 256, 256), pl.multiple_of((1 - core) * 256, 256)
    a_init = []
    for h in range(2):
        a_init.append(remote(
            h, go_ref.at[pl.ds(theirs, 256), lane_half[h]],
            ag.at[zh, core * 2 + h, pl.ds(theirs, 256)], c, partner,
        ))
    own_lanes = pl.ds(pl.multiple_of(zl * 128, 128), 128)
    wz = remote(OFF_W, w_ref, wg.at[x, y, :, own_lanes], z_peer, t)
    local = [
        pltpu.make_async_copy(
            go_ref.at[:, lane_half[h]], ag.at[zh, core * 2 + h], loc.at[h]
        )
        for h in range(2)
    ]
    local.append(pltpu.make_async_copy(w_ref, wg.at[x, y, :, own_lanes], loc.at[2]))
    for copy in local:
        copy.start()
    for h in range(2):
        a_init.append(remote(
            2 + h, go_ref.at[pl.ds(mine, 256), lane_half[h]],
            ag.at[zh, core * 2 + h, pl.ds(mine, 256)], c, partner,
        ))

    rate_rows = jnp.exp(rate2[...])
    decay_rows = jnp.exp(-rate_rows)
    amp_rows = gain2[...] * jnp.sqrt(2.0 * rate_rows)
    for m in range(MODES):
        rate3[m] = rate_rows[m:m + 1, :]
        a8[m] = jnp.broadcast_to(decay_rows[m:m + 1, :], (SUB, CH))
        amp8[m] = jnp.broadcast_to(amp_rows[m:m + 1, :], (SUB, CH))

    order = [yo, yp, ym, y]
    duty = pl.ds(mine, 256)
    duty_lo = pl.ds(mine, 128)
    duty_hi = pl.ds(pl.multiple_of(core * 256 + 128, 128), 128)
    piece_own, piece_fwd, piece_par = {}, {}, {}

    def piece_start(k):
        src = ag.at[zh, order[k], duty]
        base = 4 + 8 * k
        piece_own[k] = (
            remote(base, src, src, c, t_right), remote(base + 1, src, src, c, t_left)
        )

    def piece_forward(k):
        base = 4 + 8 * k
        from_left, from_right = piece_own[k]
        yk = order[k]
        from_left.wait_recv()
        lo = ag.at[zm, yk, duty_lo]
        f_r = remote(base + 2, lo, lo, c, t_right)
        full = ag.at[zm, yk, duty]
        p_l = remote(base + 4, full, full, c, partner)
        from_right.wait_recv()
        hi = ag.at[zp, yk, duty_hi]
        f_l = remote(base + 3, hi, hi, c, t_left)
        full = ag.at[zp, yk, duty]
        p_r = remote(base + 5, full, full, c, partner)
        piece_fwd[k] = (f_r, f_l)
        piece_par[k] = [p_l, p_r]
        if k + 2 < 4:
            piece_start(k + 2)

    def piece_end(k):
        base = 4 + 8 * k
        yk = order[k]
        f_r, f_l = piece_fwd[k]
        f_r.wait_recv()
        lo = ag.at[zo, yk, duty_lo]
        p_a = remote(base + 6, lo, lo, c, partner)
        f_l.wait_recv()
        hi = ag.at[zo, yk, duty_hi]
        p_b = remote(base + 7, hi, hi, c, partner)
        for copy in piece_par[k] + [p_a, p_b]:
            copy.wait_recv()

    for copy in local:
        copy.wait()
    for copy in a_init:
        copy.wait_recv()
    piece_start(0)

    row_id = lax.broadcasted_iota(jnp.int32, (ROWS, ROWS), 0)
    col_id = lax.broadcasted_iota(jnp.int32, (ROWS, ROWS), 1)
    perm[...] = jnp.where(col_id == STEPS * (row_id % SUB) + row_id // SUB, 1.0, 0.0).astype(BF16)
    perm_t[...] = jnp.where(row_id == STEPS * (col_id % SUB) + col_id // SUB, 1.0, 0.0).astype(BF16)

    def spread(dst, natural):
        mixed = jnp.dot(perm[...], natural, preferred_element_type=F32)
        for grp in range(GROUPS):
            dst[grp] = mixed[:, grp * LANES:(grp + 1) * LANES]

    def gather_back():
        mixed = jnp.concatenate([ys[grp] for grp in range(GROUPS)], axis=1).astype(BF16)
        return jnp.dot(perm_t[...], mixed, preferred_element_type=F32)

    signal = (k_ref[...].astype(F32) * v_ref[...].astype(F32)).astype(BF16)
    spread(xs, signal)

    w0, w1 = pl.ds(0, W_SPLIT), pl.ds(W_SPLIT, CH - W_SPLIT)
    half0, half1 = W_SPLIT // 2, (CH - W_SPLIT) // 2
    w0a, w0b = pl.ds(0, half0), pl.ds(half0, half0)
    w1a, w1b = pl.ds(W_SPLIT, half1), pl.ds(W_SPLIT + half1, half1)
    wb = OFF_W + 1
    wc = {}

    def w_send(index, ref, ctx):
        return remote(wb + index, ref, ref, ctx, t)

    def w_row(b, xb):
        wc["yr", b] = w_send(4 + 4 * b, wg.at[xb, y, w0], y_right)
        wc["yl", b] = w_send(5 + 4 * b, wg.at[xb, y, w0], y_left)

    def w_row_forward(b, xb):
        wc["yr", b].wait_recv()
        wc["yfr", b] = w_send(6 + 4 * b, wg.at[xb, ym, w0a], y_right)
        wc["yl", b].wait_recv()
        wc["yfl", b] = w_send(7 + 4 * b, wg.at[xb, yp, w0b], y_left)

    def w_first():
        wz.wait_recv()
        wc["xr"] = w_send(0, wg.at[x, y, w0], x_right)
        wc["xl"] = w_send(1, wg.at[x, y, w0], x_left)
        wc["1r"] = w_send(20, wg.at[x, y, w1], y_right)
        wc["1l"] = w_send(21, wg.at[x, y, w1], y_left)
        w_row(0, x)

    def w_second():
        wc["xr"].wait_recv()
        wc["xfr"] = w_send(2, wg.at[xm, y, w0a], x_right)
        wc["xl"].wait_recv()
        wc["xfl"] = w_send(3, wg.at[xp, y, w0b], x_left)
        wc["1r"].wait_recv()
        wc["1fr"] = w_send(22, wg.at[x, ym, w1a], y_right)
        wc["1l"].wait_recv()
        wc["1fl"] = w_send(23, wg.at[x, yp, w1b], y_left)
        w_row(1, xm)
        w_row(2, xp)

    def w_third():
        wc["1fr"].wait_recv()
        wc["1fl"].wait_recv()
        wc["2r"] = w_send(24, wg.at[x, :, w1], x_right)
        wc["2l"] = w_send(25, wg.at[x, :, w1], x_left)
        w_row_forward(0, x)
        wc["xfr"].wait_recv()
        wc["xfl"].wait_recv()
        w_row(3, xo)

    def w_fourth():
        wc["2r"].wait_recv()
        wc["2fr"] = w_send(26, wg.at[xm, :, w1a], x_right)
        wc["2l"].wait_recv()
        wc["2fl"] = w_send(27, wg.at[xp, :, w1b], x_left)
        w_row_forward(1, xm)
        w_row_forward(2, xp)

    def w_fifth():
        w_row_forward(3, xo)

    def w_end():
        for b in range(4):
            wc["yfr", b].wait_recv()
            wc["yfl", b].wait_recv()
        wc["2fr"].wait_recv()
        wc["2fl"].wait_recv()

    w_first()

    def lane_at(grp):
        return pl.ds(pl.multiple_of(grp * LANES, LANES), LANES)

    def step_rows(j):
        return pl.ds(pl.multiple_of(j * SUB, SUB), SUB)

    def rates_at(grp):
        return rate3[:, :, lane_at(grp)]

    UNROLL = 4

    def forward_group(grp):
        decay = a8[:, :, lane_at(grp)]

        def step(i, carry):
            state, timed = carry
            for u in range(UNROLL):
                decayed = decay * state
                timed = decay * timed + decayed
                state = decayed + xs[grp, step_rows(i * UNROLL + u)][None]
            return (state, timed)

        zero = jnp.zeros((MODES, SUB, LANES), F32)
        state, timed = lax.fori_loop(0, STEPS // UNROLL, step, (zero, zero))
        rates = rates_at(grp)
        for power in (1, 2, 4):
            factor = jnp.exp(-rates * float(STEPS * power))
            before = shift_sub(state, power)
            timed = timed + factor * (shift_sub(timed, power) + float(STEPS * power) * before)
            state = state + factor * before
        hfs[:, :, lane_at(grp)] = shift_sub(state, 1)
        hft[:, :, lane_at(grp)] = shift_sub(timed, 1)
        scr8[grp, 0:MODES] = state
        scr8[grp, MODES:2 * MODES] = timed

    def backward_group(grp):
        decay = a8[:, :, lane_at(grp)]

        def step(i, state):
            for u in range(UNROLL):
                j = STEPS - 1 - (i * UNROLL + u)
                state = decay * state + gs[grp, step_rows(j)][None]
            return state

        state = lax.fori_loop(0, STEPS // UNROLL, step, jnp.zeros((MODES, SUB, LANES), F32))
        rates = rates_at(grp)
        for power in (1, 2, 4):
            factor = jnp.exp(-rates * float(STEPS * power))
            state = state + factor * shift_sub(state, -power)
        hbwd[:, :, lane_at(grp)] = shift_sub(state, -1)
        scr8[grp, 0:MODES] = state

    def edge_rows(count, edge):
        for grp in range(GROUPS):
            for m in range(count):
                st2[m:m + 1, grp * LANES:(grp + 1) * LANES] = scr8[grp, m, edge:edge + 1, :]

    def scan_out(src, backward, start):
        def group(grp):
            decay = a8[:, :, lane_at(grp)]
            amp = amp8[:, :, lane_at(grp)]

            def step(i, state):
                for u in range(UNROLL):
                    j = i * UNROLL + u
                    j = STEPS - 1 - j if backward else j
                    state = decay * state + src[grp, step_rows(j)][None]
                    ys[grp, step_rows(j)] = jnp.sum(amp * state, axis=0)
                return state

            lax.fori_loop(0, STEPS // UNROLL, step, start[:, :, lane_at(grp)])

        run(0, GROUPS, group)

    def exchange(src, dst, send, recv):
        def make(other, index):
            return pltpu.make_async_remote_copy(
                src_ref=src, dst_ref=dst.at[index], send_sem=send.at[other],
                recv_sem=recv.at[index], device_id=(other * 2 + zl, t), device_id_type=MESH,
            )

        return make

    def pair_copy(n, src, dst):
        return pltpu.make_async_remote_copy(
            src_ref=src, dst_ref=dst, send_sem=pair_s.at[n], recv_sem=pair_r.at[n],
            device_id=(z_peer, t), device_id_type=MESH,
        )

    chunk = float(ROWS)
    one_decay = jnp.exp(-rate_rows * chunk)
    two_decay = jnp.exp(-rate_rows * (2.0 * chunk))
    odd = zl == 1

    run(0, GROUPS, forward_group)
    edge_rows(2 * MODES, SUB - 1)
    ebuf[...] = st2[...].astype(BF16)
    e_pair = pair_copy(0, ebuf, epeer)
    e_pair.start()
    piece_start(1)
    piece_forward(0)
    w_second()
    e_pair.wait_recv()
    peer = epeer[...].astype(F32)
    own = st2[...]
    first = jnp.where(odd, peer, own)
    second = jnp.where(odd, own, peer)
    first_s, first_t = first[:MODES], first[MODES:]
    esend[0:MODES] = (second[:MODES] + one_decay * first_s).astype(BF16)
    esend[MODES:] = (second[MODES:] + one_decay * (first_t + chunk * first_s)).astype(BF16)
    e_copy = exchange(esend, eall, e_s, e_r)
    run(plane + 1, PLANE, lambda other: e_copy(other, plane).start())
    w_third()
    piece_forward(1)

    run(0, plane, lambda other: e_copy(other, other).wait_recv())

    def join_forward(j, carry):
        head_s, head_t = carry
        rows = eall[j].astype(F32)
        return (
            two_decay * head_s + rows[:MODES],
            two_decay * (head_t + 2.0 * chunk * head_s) + rows[MODES:],
        )

    zero_rows = jnp.zeros((MODES, CH), F32)
    head_s, head_t = lax.fori_loop(0, plane, join_forward, (zero_rows, zero_rows))
    head_t = jnp.where(odd, peer[MODES:] + one_decay * (head_t + chunk * head_s), head_t)
    head_s = jnp.where(odd, peer[:MODES] + one_decay * head_s, head_s)
    for m in range(MODES):
        hd3[m] = head_s[m:m + 1, :]
        hd3[MODES + m] = head_t[m:m + 1, :]

    def incoming_forward(grp):
        ids = lax.broadcasted_iota(jnp.int32, (MODES, SUB, LANES), 1).astype(F32) * float(STEPS)
        weight = jnp.exp(-rates_at(grp) * ids)
        in_s = hd3[0:MODES, :, lane_at(grp)]
        in_t = hd3[MODES:2 * MODES, :, lane_at(grp)]
        hfs[:, :, lane_at(grp)] += weight * in_s
        hft[:, :, lane_at(grp)] += weight * (in_t + ids * in_s)

    run(0, GROUPS, incoming_forward)
    scan_out(xs, False, hfs)
    cv[...] = gather_back().astype(BF16)
    gated = (q_ref[...].astype(F32) * cv[...].astype(F32)).astype(BF16).astype(F32)
    gt[...] = jnp.transpose(gated).astype(BF16)

    rings = {}

    def add_into(ref, extra):
        ref[...] = (ref[...].astype(F32) + extra.astype(F32)).astype(BF16)
        return ref

    def part_a(part):
        return pl.ds(part * 128, 128)

    def part_b(part):
        return pl.ds(256 + part * 128, 128)

    ybase = OFF_O + 24
    bbase = OFF_O + 30
    vbase = OFF_O + 36
    along = {}

    def out_piece(k):
        yk = order[k]

        def block(j):
            op[j, yk] = jnp.dot(gt[...], ag[j, yk], preferred_element_type=F32).astype(BF16)

        run(0, 4, block)

        def unit(target, part):
            return op.at[target, yk, part_a(part)]

        base = OFF_O + 6 * k
        far_r = remote(base, unit(xo, 0), oppx.at[k, 0], x_right, t)
        far_l = remote(base + 1, unit(xo, 1), oppx.at[k, 1], x_left, t)
        rings[k] = [
            unit, far_r, far_l,
            remote(base + 2, unit(xp, 1), finx.at[k, 0, 1], x_right, t),
            remote(base + 3, unit(xm, 0), finx.at[k, 1, 0], x_left, t),
        ]

        def whole(part):
            return op.at[:, yk, part_b(part)]

        if k == 0:
            along["far_r"] = remote(bbase, whole(0), oppb.at[0], y_right, t)
            along["far_l"] = remote(bbase + 1, whole(1), oppb.at[1], y_left, t)
        elif k == 1:
            along["r1"] = remote(bbase + 2, whole(1), finb.at[0, 1], y_right, t)
        elif k == 2:
            along["l0"] = remote(bbase + 4, whole(0), finb.at[1, 0], y_left, t)

    def along_right():
        along["far_r"].wait_recv()
        ref = add_into(op.at[:, order[1], part_b(0)], oppb[0])
        along["r0"] = remote(bbase + 3, ref, finb.at[0, 0], y_right, t)

    def along_left():
        along["far_l"].wait_recv()
        ref = add_into(op.at[:, order[2], part_b(1)], oppb[1])
        along["l1"] = remote(bbase + 5, ref, finb.at[1, 1], y_left, t)

    def along_own():
        for name in ("r0", "r1", "l0", "l1"):
            along[name].wait_recv()
        for part in range(2):
            rows = slice(part * 128, (part + 1) * 128)
            vcol[:, rows] = (
                op[:, y, part_b(part)].astype(F32) + finb[0, part].astype(F32)
                + finb[1, part].astype(F32)
            ).astype(BF16)

        def unit(target, part):
            return vcol.at[target, part_a(part)]

        along["ring"] = [
            unit,
            remote(vbase, unit(xo, 0), oppv.at[0], x_right, t),
            remote(vbase + 1, unit(xo, 1), oppv.at[1], x_left, t),
            remote(vbase + 2, unit(xp, 1), finv.at[0, 1], x_right, t),
            remote(vbase + 3, unit(xm, 0), finv.at[1, 0], x_left, t),
        ]

    def along_add():
        unit, far_r, far_l = along["ring"][:3]
        far_r.wait_recv()
        ref = add_into(unit(xp, 0), oppv[0])
        along["ring"].append(remote(vbase + 4, ref, finv.at[0, 0], x_right, t))
        far_l.wait_recv()
        ref = add_into(unit(xm, 1), oppv[1])
        along["ring"].append(remote(vbase + 5, ref, finv.at[1, 1], x_left, t))

    def along_last():
        for copy in along["ring"][3:]:
            copy.wait_recv()
        for part in range(2):
            rsum[256 + part * 128:256 + (part + 1) * 128] = (
                vcol[x, part * 128:(part + 1) * 128].astype(F32) + finv[0, part].astype(F32)
                + finv[1, part].astype(F32)
            )

    def out_add(k):
        unit, far_r, far_l = rings[k][:3]
        base = OFF_O + 6 * k
        far_r.wait_recv()
        ref = add_into(unit(xp, 0), oppx[k, 0])
        rings[k].append(remote(base + 4, ref, finx.at[k, 0, 0], x_right, t))
        far_l.wait_recv()
        ref = add_into(unit(xm, 1), oppx[k, 1])
        rings[k].append(remote(base + 5, ref, finx.at[k, 1, 1], x_left, t))

    def out_sum(k):
        unit = rings[k][0]
        for copy in rings[k][3:]:
            copy.wait_recv()
        return [
            unit(x, part)[...].astype(F32) + finx[k, 0, part].astype(F32)
            + finx[k, 1, part].astype(F32)
            for part in range(2)
        ]

    second_ring = {}

    def out_first():
        parts = out_sum(0)
        for part in range(2):
            vsum[0, part] = parts[part].astype(BF16)
        second_ring["far_r"] = remote(ybase, vsum.at[0, 0], oppy.at[0], y_right, t)
        second_ring["far_l"] = remote(ybase + 1, vsum.at[0, 1], oppy.at[1], y_left, t)

    def out_second():
        parts = out_sum(1)
        vsum[1, 1] = parts[1].astype(BF16)
        second_ring["r1"] = remote(ybase + 2, vsum.at[1, 1], finy.at[0, 1], y_right, t)
        second_ring["far_r"].wait_recv()
        vsum[1, 0] = (parts[0] + oppy[0].astype(F32)).astype(BF16)
        second_ring["r0"] = remote(ybase + 3, vsum.at[1, 0], finy.at[0, 0], y_right, t)

    def out_third():
        parts = out_sum(2)
        vsum[2, 0] = parts[0].astype(BF16)
        second_ring["l0"] = remote(ybase + 4, vsum.at[2, 0], finy.at[1, 0], y_left, t)
        second_ring["far_l"].wait_recv()
        vsum[2, 1] = (parts[1] + oppy[1].astype(F32)).astype(BF16)
        second_ring["l1"] = remote(ybase + 5, vsum.at[2, 1], finy.at[1, 1], y_left, t)

    def out_last():
        parts = out_sum(3)
        for name in ("r0", "r1", "l0", "l1"):
            second_ring[name].wait_recv()
        for part in range(2):
            rsum[part * 128:(part + 1) * 128] = (
                parts[part] + finy[0, part].astype(F32) + finy[1, part].astype(F32)
            )

    dims = (((1,), (1,)), ((), ()))

    def gate_piece(k):
        yk = order[k]

        def block(j):
            gate[...] += lax.dot_general(
                ag[j, yk], wg[j, yk], dims, preferred_element_type=F32
            )

        run(0, 4, block)

    w_fourth()
    piece_end(0)
    out_piece(0)
    piece_forward(2)
    w_fifth()
    piece_end(1)
    out_piece(1)
    out_add(0)
    piece_forward(3)
    along_right()
    gate[...] = jnp.zeros_like(gate)
    w_end()
    gate_piece(0)
    gate_piece(1)
    out_first()
    piece_end(2)
    out_piece(2)
    out_add(1)
    gate_piece(2)
    along_left()
    piece_end(3)
    gate_piece(3)

    conv_grad = (gate[...] * q_ref[...].astype(F32)).astype(BF16)
    spread(gs, conv_grad)
    run(0, GROUPS, backward_group)
    edge_rows(MODES, 0)
    qbuf[...] = st2[0:MODES].astype(BF16)
    q_pair = pair_copy(1, qbuf, qpeer)
    q_pair.start()
    q_pair.wait_recv()
    peer_q = qpeer[...].astype(F32)
    own_q = st2[0:MODES]
    first_q = jnp.where(odd, peer_q, own_q)
    second_q = jnp.where(odd, own_q, peer_q)
    qsend[...] = (first_q + one_decay * second_q).astype(BF16)
    q_copy = exchange(qsend, qall, q_s, q_r)
    run(0, plane, lambda other: q_copy(other, plane).start())

    out_piece(3)
    out_add(2)
    along_own()
    gq_out[...] = (gate[...] * cv[...].astype(F32)).astype(BF16)

    def gain_scan(grp):
        for part in range(2):
            mode = pl.ds(part * 8, 8)
            decay = a8[mode, :, lane_at(grp)]

            def step(i, carry):
                state, timed, gain_sum, rate_sum = carry
                for u in range(UNROLL):
                    rows = step_rows(i * UNROLL + u)
                    grad = gs[grp, rows][None]
                    decayed = decay * state
                    timed = decay * timed + decayed
                    state = decayed + xs[grp, rows][None]
                    gain_sum = gain_sum + grad * state
                    rate_sum = rate_sum + grad * timed
                return (state, timed, gain_sum, rate_sum)

            zero = jnp.zeros((8, SUB, LANES), F32)
            _, _, gain_sum, rate_sum = lax.fori_loop(
                0, STEPS // UNROLL, step,
                (hfs[mode, :, lane_at(grp)], hft[mode, :, lane_at(grp)], zero, zero),
            )
            scr8[grp, mode] = gain_sum
            scr8[grp, pl.ds(MODES + part * 8, 8)] = rate_sum

    out_second()
    run(0, GROUPS, gain_scan)
    for grp in range(GROUPS):
        yz[:, grp] = jnp.sum(scr8[grp], axis=1)

    def y_copy(d, index):
        other = (c + d) % NCTX
        return pltpu.make_async_remote_copy(
            src_ref=yz.at[other], dst_ref=yz_in.at[index], send_sem=y_s.at[other],
            recv_sem=y_r.at[index], device_id=(other, t), device_id_type=MESH,
        )

    run(1, NCTX, lambda d: y_copy(d, c).start())
    out_add(3)
    along_add()
    for copy in pending[:OFF_O]:
        copy.wait_send()

    run(plane + 1, PLANE, lambda other: q_copy(other, other).wait_recv())
    tail = lax.fori_loop(
        0, PLANE - 1 - plane,
        lambda j, h: two_decay * h + qall[PLANE - 1 - j].astype(F32),
        zero_rows,
    )
    tail = jnp.where(odd, tail, peer_q + one_decay * tail)
    for m in range(MODES):
        hd3[m] = tail[m:m + 1, :]

    def incoming_backward(grp):
        ids = lax.broadcasted_iota(jnp.int32, (MODES, SUB, LANES), 1).astype(F32)
        weight = jnp.exp(-rates_at(grp) * (((SUB - 1.0) - ids) * float(STEPS)))
        hbwd[:, :, lane_at(grp)] += weight * hd3[0:MODES, :, lane_at(grp)]

    run(0, GROUPS, incoming_backward)
    out_third()
    scan_out(gs, True, hbwd)

    run(1, NCTX, lambda d: y_copy(d, (c + d) % NCTX).wait_recv())
    yz_in[c] = yz[c]
    yz_all[c] = jnp.sum(yz_in[...], axis=0)

    def o_copy(d, index):
        other = (c + d) % NCTX
        return pltpu.make_async_remote_copy(
            src_ref=yz_all.at[c], dst_ref=yz_all.at[index], send_sem=o_s.at[other],
            recv_sem=o_r.at[index], device_id=(other, t), device_id_type=MESH,
        )

    run(1, NCTX, lambda d: o_copy(d, c).start())

    out_last()
    along_last()
    rsend[...] = rsum[:, pl.ds(pl.multiple_of((1 - zl) * 128, 128), 128)].astype(BF16)
    z_copy = remote(OFF_O + 42, rsend, zin, z_peer, t)

    input_grad = gather_back().astype(BF16).astype(F32)
    gk_out[...] = (input_grad * v_ref[...].astype(F32)).astype(BF16)
    gv_out[...] = (input_grad * k_ref[...].astype(F32)).astype(BF16)

    z_copy.wait_recv()
    ow_out[...] = (rsum[:, own_lanes] + zin[...].astype(F32)) * NORM

    run(1, NCTX, lambda d: o_copy(d, (c + d) % NCTX).wait_recv())
    scale = NORM * jnp.sqrt(2.0 * rate_rows)
    gain_sum = jnp.concatenate([yz_all[0:MODES, grp] for grp in range(GROUPS)], axis=1)
    rate_sum = jnp.concatenate([yz_all[MODES:2 * MODES, grp] for grp in range(GROUPS)], axis=1)
    gain_out[...] = scale * gain_sum
    rate_out[...] = scale * gain2[...] * (0.5 * gain_sum - rate_rows * rate_sum)
    e_pair.wait_send()
    q_pair.wait_send()
    run(plane + 1, PLANE, lambda other: e_copy(other, plane).wait_send())
    run(0, plane, lambda other: q_copy(other, plane).wait_send())
    run(1, NCTX, lambda d: y_copy(d, c).wait_send())
    run(1, NCTX, lambda d: o_copy(d, c).wait_send())
    for copy in pending[OFF_O:]:
        copy.wait_send()


def on_device(query_proj, key_proj, value_proj, filter_gains, log_rates, out_weight, grad_out):
    gain2 = filter_gains.T
    rate2 = log_rates.T
    vmem = pl.BlockSpec(memory_space=pltpu.VMEM)
    shape = jax.ShapeDtypeStruct
    dma = pltpu.SemaphoreType.DMA
    wide = (MODES, SUB, CH)
    grad_query, grad_key, grad_value, grad_gains, grad_rates, grad_weight = pl.pallas_call(
        kernel,
        out_shape=(
            shape((ROWS, CH), BF16),
            shape((ROWS, CH), BF16),
            shape((ROWS, CH), BF16),
            shape((MODES, CH), F32),
            shape((MODES, CH), F32),
            shape((CH, 128), F32),
        ),
        in_specs=[vmem] * 7,
        out_specs=[vmem] * 6,
        scratch_shapes=[
            pltpu.VMEM((MODES, 1, CH), F32),
            pltpu.VMEM((4, 4, ROWS, 256), BF16),
            pltpu.VMEM((4, 4, CH, 256), BF16),
            pltpu.VMEM((4, 4, CH, 256), BF16),
            pltpu.VMEM((GROUPS, ROWS, LANES), F32),
            pltpu.VMEM((GROUPS, ROWS, LANES), F32),
            pltpu.VMEM((GROUPS, ROWS, LANES), F32),
            pltpu.VMEM((ROWS, ROWS), BF16),
            pltpu.VMEM((ROWS, ROWS), BF16),
            pltpu.VMEM(wide, F32),
            pltpu.VMEM(wide, F32),
            pltpu.VMEM((2 * MODES, CH), BF16),
            pltpu.VMEM((2 * MODES, CH), BF16),
            pltpu.VMEM((2 * MODES, CH), BF16),
            pltpu.VMEM((PLANE, 2 * MODES, CH), BF16),
            pltpu.VMEM((MODES, CH), BF16),
            pltpu.VMEM((MODES, CH), BF16),
            pltpu.VMEM((MODES, CH), BF16),
            pltpu.VMEM((PLANE, MODES, CH), BF16),
            pltpu.VMEM((2 * MODES, 1, CH), F32),
            pltpu.VMEM((2 * MODES, CH), F32),
            pltpu.VMEM((GROUPS, 2 * MODES, SUB, LANES), F32),
            pltpu.VMEM(wide, F32),
            pltpu.VMEM(wide, F32),
            pltpu.VMEM(wide, F32),
            pltpu.VMEM((ROWS, CH), F32),
            pltpu.VMEM((ROWS, CH), BF16),
            pltpu.VMEM((CH, ROWS), BF16),
            pltpu.VMEM((2 * MODES, GROUPS, LANES), F32),
            pltpu.VMEM((NCTX, GROUPS, LANES), F32),
            pltpu.VMEM((NCTX, GROUPS, LANES), F32),
            pltpu.VMEM((4, 2, 128, 256), BF16),
            pltpu.VMEM((4, 2, 2, 128, 256), BF16),
            pltpu.VMEM((3, 2, 128, 256), BF16),
            pltpu.VMEM((2, 128, 256), BF16),
            pltpu.VMEM((2, 2, 128, 256), BF16),
            pltpu.VMEM((2, 4, 128, 256), BF16),
            pltpu.VMEM((2, 2, 4, 128, 256), BF16),
            pltpu.VMEM((4, 256, 256), BF16),
            pltpu.VMEM((2, 128, 256), BF16),
            pltpu.VMEM((2, 2, 128, 256), BF16),
            pltpu.VMEM((CH, 256), F32),
            pltpu.VMEM((CH, 128), BF16),
            pltpu.VMEM((CH, 128), BF16),
            dma((N_RING,)),
            dma((N_RING,)),
            dma((PLANE,)),
            dma((PLANE,)),
            dma((PLANE,)),
            dma((PLANE,)),
            dma((NCTX,)),
            dma((NCTX,)),
            dma((NCTX,)),
            dma((NCTX,)),
            dma((2,)),
            dma((2,)),
            dma((3,)),
        ],
        compiler_params=pltpu.CompilerParams(
            collective_id=0, has_side_effects=True, vmem_limit_bytes=56 * 1024 * 1024
        ),
        cost_estimate=pl.CostEstimate(
            flops=5_000_000_000, bytes_accessed=5_000_000, transcendentals=0
        ),
    )(
        query_proj, key_proj, value_proj, gain2, rate2, out_weight, grad_out,
    )
    return (grad_query, grad_key, grad_value, grad_gains.T, grad_rates.T, grad_weight)


def solution(mesh):
    in_specs = (
        P("context", "tensor"),
        P("context", "tensor"),
        P("context", "tensor"),
        P("tensor", None),
        P("tensor", None),
        P("tensor", "context"),
        P("context", "tensor"),
    )
    out_specs = (
        P("context", "tensor"),
        P("context", "tensor"),
        P("context", "tensor"),
        P("tensor", None),
        P("tensor", None),
        P("tensor", "context"),
    )
    return jax.shard_map(
        on_device, mesh=mesh, in_specs=in_specs, out_specs=out_specs, check_vma=False
    )
```

time: 126 us -> 104 us (0.83); the launches traced: 126 us -> 102 us
  Pallas kernels: 117 us -> 95.7 us
  local copies, waits for them, and re-layouts: 7.86 us -> 6.05 us
    pallas_call x1, Pallas kernels: 117 us -> 95.7 us  [on_device(): pl.pallas_call(kernel, out_shape=(shape((ROWS, CH), BF16), shape((ROWS, C...]
    broadcast_in_dim x2 -> x0, local copies, waits for them, and re-layouts: 2.04 us -> none  [the longest x1 1.4 us: on_device(): gain2[:, None, :]]
    unnamed x17 -> x16, local copies, waits for them, and re-layouts: 5.83 us -> 6.05 us
where the time goes in v2:
time: 104 us; the launch traced here: 102 us
  Pallas kernels  95.7 us (92%)
  local copies, waits for them, and re-layouts  6.05 us (6%)
    pallas_call x1, Pallas kernels, on_device(): pl.pallas_call(kernel, out_shape=(shape((ROWS, CH), BF16), shape((ROWS, C...  95.7 us
    unnamed x16, local copies, waits for them, and re-layouts  6.05 us

profile of v2, /device:TPU:32, one launch (start us, length us, event | category | flops | bytes accessed | tf_op | source)
XLA Modules:
  0.0 102.4 jit_solution(7711575786752296887)
XLA Ops:
  0.6 95.7 %shard_map.118 = (bf16[512,512]{1,0:T(8,128)(2,1)}, bf16[512,512]{1,0:T(8,128)(2,1)}, bf16[512,512]{1,0:T(8,128)(2,1)}, f32[16,512]{1,0:T(8,128)}, f32[16,512]{1,0:T(8,128)}, /*index=5*/f32[512,128]{1,0:T(8,128)}) custom-call(bf16[512,512]{1,0:T(8,128)(2,1)} %q_ref.1, bf16[512,512]{1,0:T(8,128)(2,1)} %k_ref.1, bf16[512,512]{1,0:T(8,128)(2,1)} %v_ref.1, ...), custom_call_target="tpu_custom_call" | custom-call | flops 5000000000 | bytes 5000000 | tf_op jit(solution)/shard_map/pallas_call | solution.py:735
  96.4 0.0 copy-start.1
  96.4 1.9 %copy.19 = bf16[512,512]{1,0:T(8,128)(2,1)} copy(bf16[512,512]{1,0:T(8,128)(2,1)} %get-tuple-element.24) | data formatting | bytes 1048576
  98.3 0.0 copy-done.1
  98.3 0.0 copy-start
  98.3 0.8 copy.20
  99.1 0.4 copy-done
  99.5 0.0 copy-start.4
  99.5 0.0 copy-start.2
  99.5 0.8 copy.21
  100.3 0.0 copy-done.4
  100.3 0.0 copy-start.3
  100.3 0.6 copy.22
  101.0 0.2 copy-done.3
  101.1 0.6 copy.23
  101.7 0.0 copy-done.2
  101.7 0.7 copy.24
Async XLA Ops:
  96.4 1.9 %copy-start.1 = (bf16[512,512]{1,0:T(8,128)(2,1)S(1)}, bf16[512,512]{1,0:T(8,128)(2,1)}, u32[]{:S(2)}) copy-start(bf16[512,512]{1,0:T(8,128)(2,1)} %get-tuple-element.25) | copy-start | bytes 1572868
  98.3 1.2 %copy-start = (bf16[512,512]{1,0:T(8,128)(2,1)S(1)}, bf16[512,512]{1,0:T(8,128)(2,1)}, u32[]{:S(2)}) copy-start(bf16[512,512]{1,0:T(8,128)(2,1)} %get-tuple-element.26) | copy-start | bytes 1572868
  99.5 0.8 copy-start.4
  99.5 2.2 %copy-start.2 = (f32[512,128]{1,0:T(8,128)S(1)}, f32[512,128]{1,0:T(8,128)}, u32[]{:S(2)}) copy-start(f32[512,128]{1,0:T(8,128)} %get-tuple-element.29) | copy-start | bytes 786436
  100.3 0.8 copy-start.3

commit v3 on v2

--- a/solution.py
+++ b/solution.py
@@ -23,11 +23,12 @@
 NORM = 1.0 / math.sqrt(SEQ)
 
 N_A = 36
-N_W = 29
+N_W = 45
 N_O = 6 * 4 + 6 + 6 + 6 + 1
 OFF_W = N_A
 OFF_O = OFF_W + N_W
 N_RING = OFF_O + N_O
+SENT_ROWS = (448, 496, 496)
 PLANE = 16
 W_SPLIT = 256
 
@@ -40,13 +41,13 @@
 
 
 def kernel(
-    q_ref, k_ref, v_ref, gain2, rate2, w_ref, go_ref,
+    q_in, k_in, v_in, gain2, rate2, w_ref, go_ref,
     gq_out, gk_out, gv_out, gain_out, rate_out, ow_out,
-    rate3, ag, wg, op, xs, gs, ys, perm, perm_t, a8, amp8,
+    q_ref, k_ref, v_ref, gq_buf, gk_buf, gv_buf, ow_buf, rate3, ag, wg, op, xs, gs, ys, perm, perm_t, a8, amp8,
     ebuf, epeer, esend, eall, qbuf, qpeer, qsend, qall, hd3, st2,
     scr8, hfs, hft, hbwd, gate, cv, gt, yz, yz_in, yz_all,
     oppx, finx, vsum, oppy, finy, oppb, finb, vcol, oppv, finv, rsum, rsend, zin,
-    ring_s, ring_r, e_s, e_r, q_s, q_r, y_s, y_r, o_s, o_r, pair_s, pair_r, loc,
+    ring_s, ring_r, e_s, e_r, q_s, q_r, y_s, y_r, o_s, o_r, pair_s, pair_r, loc, io,
 ):
     c = lax.axis_index("context")
     t = lax.axis_index("tensor")
@@ -69,16 +70,17 @@
     partner = zh * 2 + (1 - core)
     t_right, t_left = zp * 2 + core, zm * 2 + core
 
-    pending = []
-
     def remote(index, src, dst, ctx, ten):
         copy = pltpu.make_async_remote_copy(
-            src_ref=src, dst_ref=dst, send_sem=ring_s.at[index], recv_sem=ring_r.at[index],
+            src_ref=src, dst_ref=dst, send_sem=ring_s.at[(index >= OFF_W) + (index >= OFF_O)],
+            recv_sem=ring_r.at[index],
             device_id=(ctx, ten), device_id_type=MESH,
         )
         copy.start()
-        pending.append(copy)
         return copy
+
+    def wait_bytes(ref, sem):
+        pltpu.make_async_copy(ref, ref, sem).wait()
 
     def run(first, last, fun):
         def body(i, carry):
@@ -95,6 +97,13 @@
     run(1, NCTX, greet)
     for ten in (partner, t_right, t_left):
         pl.semaphore_signal(barrier, inc=1, device_id=(c, ten), device_id_type=MESH)
+    loads = [
+        pltpu.make_async_copy(src, dst, io.at[n])
+        for n, (src, dst) in enumerate([(k_in, k_ref), (v_in, v_ref), (q_in, q_ref)])
+    ]
+    for copy in loads:
+        copy.start()
+
     pl.semaphore_wait(barrier, NCTX - 1 + 3)
 
     lane_half = [pl.ds(0, 256), pl.ds(256, 256)]
@@ -122,14 +131,6 @@
             ag.at[zh, core * 2 + h, pl.ds(mine, 256)], c, partner,
         ))
 
-    rate_rows = jnp.exp(rate2[...])
-    decay_rows = jnp.exp(-rate_rows)
-    amp_rows = gain2[...] * jnp.sqrt(2.0 * rate_rows)
-    for m in range(MODES):
-        rate3[m] = rate_rows[m:m + 1, :]
-        a8[m] = jnp.broadcast_to(decay_rows[m:m + 1, :], (SUB, CH))
-        amp8[m] = jnp.broadcast_to(amp_rows[m:m + 1, :], (SUB, CH))
-
     order = [yo, yp, ym, y]
     duty = pl.ds(mine, 256)
     duty_lo = pl.ds(mine, 128)
@@ -162,7 +163,7 @@
         if k + 2 < 4:
             piece_start(k + 2)
 
-    def piece_end(k):
+    def piece_pass(k):
         base = 4 + 8 * k
         yk = order[k]
         f_r, f_l = piece_fwd[k]
@@ -172,19 +173,19 @@
         f_l.wait_recv()
         hi = ag.at[zo, yk, duty_hi]
         p_b = remote(base + 7, hi, hi, c, partner)
-        for copy in piece_par[k] + [p_a, p_b]:
+        piece_par[k] += [p_a, p_b]
+
+    def piece_wait(k):
+        for copy in piece_par[k]:
             copy.wait_recv()
 
-    for copy in local:
-        copy.wait()
-    for copy in a_init:
-        copy.wait_recv()
-    piece_start(0)
-
-    row_id = lax.broadcasted_iota(jnp.int32, (ROWS, ROWS), 0)
-    col_id = lax.broadcasted_iota(jnp.int32, (ROWS, ROWS), 1)
-    perm[...] = jnp.where(col_id == STEPS * (row_id % SUB) + row_id // SUB, 1.0, 0.0).astype(BF16)
-    perm_t[...] = jnp.where(row_id == STEPS * (col_id % SUB) + col_id // SUB, 1.0, 0.0).astype(BF16)
+    rate_rows = jnp.exp(rate2[...])
+    decay_rows = jnp.exp(-rate_rows)
+    amp_rows = gain2[...] * jnp.sqrt(2.0 * rate_rows)
+    for m in range(MODES):
+        rate3[m] = rate_rows[m:m + 1, :]
+        a8[m] = jnp.broadcast_to(decay_rows[m:m + 1, :], (SUB, CH))
+        amp8[m] = jnp.broadcast_to(amp_rows[m:m + 1, :], (SUB, CH))
 
     def spread(dst, natural):
         mixed = jnp.dot(perm[...], natural, preferred_element_type=F32)
@@ -194,9 +195,6 @@
     def gather_back():
         mixed = jnp.concatenate([ys[grp] for grp in range(GROUPS)], axis=1).astype(BF16)
         return jnp.dot(perm_t[...], mixed, preferred_element_type=F32)
-
-    signal = (k_ref[...].astype(F32) * v_ref[...].astype(F32)).astype(BF16)
-    spread(xs, signal)
 
     w0, w1 = pl.ds(0, W_SPLIT), pl.ds(W_SPLIT, CH - W_SPLIT)
     half0, half1 = W_SPLIT // 2, (CH - W_SPLIT) // 2
@@ -218,15 +216,35 @@
         wc["yl", b].wait_recv()
         wc["yfl", b] = w_send(7 + 4 * b, wg.at[xb, yp, w0b], y_left)
 
+    def w_col(b, yb):
+        wc["xr", b] = w_send(24 + 4 * b, wg.at[x, yb, w1], x_right)
+        wc["xl", b] = w_send(25 + 4 * b, wg.at[x, yb, w1], x_left)
+
+    def w_col_forward(b, yb):
+        wc["xr", b].wait_recv()
+        wc["xfr", b] = w_send(26 + 4 * b, wg.at[xm, yb, w1a], x_right)
+        wc["xl", b].wait_recv()
+        wc["xfl", b] = w_send(27 + 4 * b, wg.at[xp, yb, w1b], x_left)
+
+    def w_early():
+        for n, (rows, ctx) in enumerate(((w0, x_right), (w0, x_left), (w1, y_right), (w1, y_left))):
+            wc["early", n] = remote(
+                wb + 40 + n, w_ref.at[rows], wg.at[x, y, rows, own_lanes], ctx, t
+            )
+
     def w_first():
         wz.wait_recv()
-        wc["xr"] = w_send(0, wg.at[x, y, w0], x_right)
-        wc["xl"] = w_send(1, wg.at[x, y, w0], x_left)
-        wc["1r"] = w_send(20, wg.at[x, y, w1], y_right)
-        wc["1l"] = w_send(21, wg.at[x, y, w1], y_left)
+        peer_lanes = pl.ds(pl.multiple_of((1 - zl) * 128, 128), 128)
+        wc["xr"] = w_send(0, wg.at[x, y, w0, peer_lanes], x_right)
+        wc["xl"] = w_send(1, wg.at[x, y, w0, peer_lanes], x_left)
+        wc["1r"] = w_send(20, wg.at[x, y, w1, peer_lanes], y_right)
+        wc["1l"] = w_send(21, wg.at[x, y, w1, peer_lanes], y_left)
         w_row(0, x)
+        w_col(0, y)
 
     def w_second():
+        for n in range(4):
+            wc["early", n].wait_recv()
         wc["xr"].wait_recv()
         wc["xfr"] = w_send(2, wg.at[xm, y, w0a], x_right)
         wc["xl"].wait_recv()
@@ -236,37 +254,36 @@
         wc["1l"].wait_recv()
         wc["1fl"] = w_send(23, wg.at[x, yp, w1b], y_left)
         w_row(1, xm)
+        w_col(1, ym)
         w_row(2, xp)
+        w_col(2, yp)
 
     def w_third():
         wc["1fr"].wait_recv()
         wc["1fl"].wait_recv()
-        wc["2r"] = w_send(24, wg.at[x, :, w1], x_right)
-        wc["2l"] = w_send(25, wg.at[x, :, w1], x_left)
-        w_row_forward(0, x)
         wc["xfr"].wait_recv()
         wc["xfl"].wait_recv()
         w_row(3, xo)
+        w_col(3, yo)
+        w_row_forward(0, x)
+        w_col_forward(0, y)
 
     def w_fourth():
-        wc["2r"].wait_recv()
-        wc["2fr"] = w_send(26, wg.at[xm, :, w1a], x_right)
-        wc["2l"].wait_recv()
-        wc["2fl"] = w_send(27, wg.at[xp, :, w1b], x_left)
         w_row_forward(1, xm)
+        w_col_forward(1, ym)
         w_row_forward(2, xp)
+        w_col_forward(2, yp)
 
     def w_fifth():
         w_row_forward(3, xo)
+        w_col_forward(3, yo)
 
     def w_end():
         for b in range(4):
-            wc["yfr", b].wait_recv()
-            wc["yfl", b].wait_recv()
-        wc["2fr"].wait_recv()
-        wc["2fl"].wait_recv()
-
-    w_first()
+            for name in ("yfr", "yfl", "xfr", "xfl"):
+                wc[name, b].wait_recv()
+
+    w_early()
 
     def lane_at(grp):
         return pl.ds(pl.multiple_of(grp * LANES, LANES), LANES)
@@ -325,7 +342,7 @@
             for m in range(count):
                 st2[m:m + 1, grp * LANES:(grp + 1) * LANES] = scr8[grp, m, edge:edge + 1, :]
 
-    def scan_out(src, backward, start):
+    def scan_out(src, backward, start, group0, group1):
         def group(grp):
             decay = a8[:, :, lane_at(grp)]
             amp = amp8[:, :, lane_at(grp)]
@@ -340,7 +357,7 @@
 
             lax.fori_loop(0, STEPS // UNROLL, step, start[:, :, lane_at(grp)])
 
-        run(0, GROUPS, group)
+        run(group0, group1, group)
 
     def exchange(src, dst, send, recv):
         def make(other, index):
@@ -362,13 +379,28 @@
     two_decay = jnp.exp(-rate_rows * (2.0 * chunk))
     odd = zl == 1
 
-    run(0, GROUPS, forward_group)
+    for copy in local:
+        copy.wait()
+    for copy in a_init:
+        copy.wait_recv()
+    piece_start(0)
+    row_id = lax.broadcasted_iota(jnp.int32, (ROWS, ROWS), 0)
+    col_id = lax.broadcasted_iota(jnp.int32, (ROWS, ROWS), 1)
+    perm[...] = jnp.where(col_id == STEPS * (row_id % SUB) + row_id // SUB, 1.0, 0.0).astype(BF16)
+    perm_t[...] = jnp.where(row_id == STEPS * (col_id % SUB) + col_id // SUB, 1.0, 0.0).astype(BF16)
+
+    loads[0].wait()
+    loads[1].wait()
+    signal = (k_ref[...].astype(F32) * v_ref[...].astype(F32)).astype(BF16)
+    spread(xs, signal)
+    run(0, 2, forward_group)
+    w_first()
+    run(2, GROUPS, forward_group)
     edge_rows(2 * MODES, SUB - 1)
     ebuf[...] = st2[...].astype(BF16)
     e_pair = pair_copy(0, ebuf, epeer)
     e_pair.start()
     piece_start(1)
-    piece_forward(0)
     w_second()
     e_pair.wait_recv()
     peer = epeer[...].astype(F32)
@@ -380,6 +412,7 @@
     esend[MODES:] = (second[MODES:] + one_decay * (first_t + chunk * first_s)).astype(BF16)
     e_copy = exchange(esend, eall, e_s, e_r)
     run(plane + 1, PLANE, lambda other: e_copy(other, plane).start())
+    piece_forward(0)
     w_third()
     piece_forward(1)
 
@@ -410,7 +443,13 @@
         hft[:, :, lane_at(grp)] += weight * (in_t + ids * in_s)
 
     run(0, GROUPS, incoming_forward)
-    scan_out(xs, False, hfs)
+    w_fourth()
+    scan_out(xs, False, hfs, 0, 2)
+    piece_pass(0)
+    scan_out(xs, False, hfs, 2, GROUPS)
+    w_fifth()
+    piece_forward(2)
+    loads[2].wait()
     cv[...] = gather_back().astype(BF16)
     gated = (q_ref[...].astype(F32) * cv[...].astype(F32)).astype(BF16).astype(F32)
     gt[...] = jnp.transpose(gated).astype(BF16)
@@ -578,28 +617,28 @@
 
         run(0, 4, block)
 
-    w_fourth()
-    piece_end(0)
+    piece_pass(1)
+    piece_wait(0)
     out_piece(0)
-    piece_forward(2)
-    w_fifth()
-    piece_end(1)
+    w_end()
+    gate[...] = jnp.zeros_like(gate)
+    gate_piece(0)
+    piece_forward(3)
+    piece_wait(1)
     out_piece(1)
+    gate_piece(1)
     out_add(0)
-    piece_forward(3)
+    piece_pass(2)
     along_right()
-    gate[...] = jnp.zeros_like(gate)
-    w_end()
-    gate_piece(0)
-    gate_piece(1)
-    out_first()
-    piece_end(2)
+    piece_wait(2)
     out_piece(2)
     out_add(1)
     gate_piece(2)
+    piece_pass(3)
     along_left()
-    piece_end(3)
+    piece_wait(3)
     gate_piece(3)
+    out_first()
 
     conv_grad = (gate[...] * q_ref[...].astype(F32)).astype(BF16)
     spread(gs, conv_grad)
@@ -608,19 +647,6 @@
     qbuf[...] = st2[0:MODES].astype(BF16)
     q_pair = pair_copy(1, qbuf, qpeer)
     q_pair.start()
-    q_pair.wait_recv()
-    peer_q = qpeer[...].astype(F32)
-    own_q = st2[0:MODES]
-    first_q = jnp.where(odd, peer_q, own_q)
-    second_q = jnp.where(odd, own_q, peer_q)
-    qsend[...] = (first_q + one_decay * second_q).astype(BF16)
-    q_copy = exchange(qsend, qall, q_s, q_r)
-    run(0, plane, lambda other: q_copy(other, plane).start())
-
-    out_piece(3)
-    out_add(2)
-    along_own()
-    gq_out[...] = (gate[...] * cv[...].astype(F32)).astype(BF16)
 
     def gain_scan(grp):
         for part in range(2):
@@ -647,23 +673,50 @@
             scr8[grp, mode] = gain_sum
             scr8[grp, pl.ds(MODES + part * 8, 8)] = rate_sum
 
-    out_second()
-    run(0, GROUPS, gain_scan)
-    for grp in range(GROUPS):
-        yz[:, grp] = jnp.sum(scr8[grp], axis=1)
-
     def y_copy(d, index):
         other = (c + d) % NCTX
         return pltpu.make_async_remote_copy(
-            src_ref=yz.at[other], dst_ref=yz_in.at[index], send_sem=y_s.at[other],
-            recv_sem=y_r.at[index], device_id=(other, t), device_id_type=MESH,
+            src_ref=yz.at[other], dst_ref=yz_in.at[index], send_sem=y_s.at[0],
+            recv_sem=y_r.at[0], device_id=(other, t), device_id_type=MESH,
         )
 
+    def o_copy(d, index):
+        other = (c + d) % NCTX
+        return pltpu.make_async_remote_copy(
+            src_ref=yz_all.at[c], dst_ref=yz_all.at[index], send_sem=o_s.at[0],
+            recv_sem=o_r.at[0], device_id=(other, t), device_id_type=MESH,
+        )
+
+    def incoming_backward(grp):
+        ids = lax.broadcasted_iota(jnp.int32, (MODES, SUB, LANES), 1).astype(F32)
+        weight = jnp.exp(-rates_at(grp) * (((SUB - 1.0) - ids) * float(STEPS)))
+        hbwd[:, :, lane_at(grp)] += weight * hd3[0:MODES, :, lane_at(grp)]
+
+    out_piece(3)
+    out_add(2)
+    q_pair.wait_recv()
+    peer_q = qpeer[...].astype(F32)
+    own_q = st2[0:MODES]
+    first_q = jnp.where(odd, peer_q, own_q)
+    second_q = jnp.where(odd, own_q, peer_q)
+    qsend[...] = (first_q + one_decay * second_q).astype(BF16)
+    q_copy = exchange(qsend, qall, q_s, q_r)
+    run(0, plane, lambda other: q_copy(other, plane).start())
+
+    gq_buf[...] = (gate[...] * cv[...].astype(F32)).astype(BF16)
+    stores = [pltpu.make_async_copy(gq_buf, gq_out, io.at[3])]
+    stores[0].start()
+    out_second()
+    along_own()
+    run(0, 1, gain_scan)
+    out_add(3)
+    run(1, 3, gain_scan)
+    out_third()
+    run(3, GROUPS, gain_scan)
+    for grp in range(GROUPS):
+        yz[:, grp] = jnp.sum(scr8[grp], axis=1)
     run(1, NCTX, lambda d: y_copy(d, c).start())
-    out_add(3)
     along_add()
-    for copy in pending[:OFF_O]:
-        copy.wait_send()
 
     run(plane + 1, PLANE, lambda other: q_copy(other, other).wait_recv())
     tail = lax.fori_loop(
@@ -674,61 +727,56 @@
     tail = jnp.where(odd, tail, peer_q + one_decay * tail)
     for m in range(MODES):
         hd3[m] = tail[m:m + 1, :]
-
-    def incoming_backward(grp):
-        ids = lax.broadcasted_iota(jnp.int32, (MODES, SUB, LANES), 1).astype(F32)
-        weight = jnp.exp(-rates_at(grp) * (((SUB - 1.0) - ids) * float(STEPS)))
-        hbwd[:, :, lane_at(grp)] += weight * hd3[0:MODES, :, lane_at(grp)]
-
     run(0, GROUPS, incoming_backward)
-    out_third()
-    scan_out(gs, True, hbwd)
-
-    run(1, NCTX, lambda d: y_copy(d, (c + d) % NCTX).wait_recv())
-    yz_in[c] = yz[c]
-    yz_all[c] = jnp.sum(yz_in[...], axis=0)
-
-    def o_copy(d, index):
-        other = (c + d) % NCTX
-        return pltpu.make_async_remote_copy(
-            src_ref=yz_all.at[c], dst_ref=yz_all.at[index], send_sem=o_s.at[other],
-            recv_sem=o_r.at[index], device_id=(other, t), device_id_type=MESH,
-        )
-
-    run(1, NCTX, lambda d: o_copy(d, c).start())
-
+    scan_out(gs, True, hbwd, 0, 2)
     out_last()
     along_last()
     rsend[...] = rsum[:, pl.ds(pl.multiple_of((1 - zl) * 128, 128), 128)].astype(BF16)
     z_copy = remote(OFF_O + 42, rsend, zin, z_peer, t)
-
+    scan_out(gs, True, hbwd, 2, GROUPS)
+    wait_bytes(yz_in.at[pl.ds(0, NCTX - 1)], y_r.at[0])
+    yz_in[c] = yz[c]
+    yz_all[c] = jnp.sum(yz_in[...], axis=0)
+    run(1, NCTX, lambda d: o_copy(d, c).start())
     input_grad = gather_back().astype(BF16).astype(F32)
-    gk_out[...] = (input_grad * v_ref[...].astype(F32)).astype(BF16)
-    gv_out[...] = (input_grad * k_ref[...].astype(F32)).astype(BF16)
-
+    gk_buf[...] = (input_grad * v_ref[...].astype(F32)).astype(BF16)
+    stores.append(pltpu.make_async_copy(gk_buf, gk_out, io.at[4]))
+    stores[1].start()
+    gv_buf[...] = (input_grad * k_ref[...].astype(F32)).astype(BF16)
+    stores.append(pltpu.make_async_copy(gv_buf, gv_out, io.at[5]))
+    stores[2].start()
+
+    def flush_sends():
+        run(plane + 1, PLANE, lambda other: e_copy(other, plane).wait_send())
+        run(0, plane, lambda other: q_copy(other, plane).wait_send())
+        wait_bytes(yz.at[pl.ds(0, NCTX - 1)], y_s.at[0])
+        e_pair.wait_send()
+        q_pair.wait_send()
+        for n, (ref, rows) in enumerate(zip((ag, wg, op), SENT_ROWS)):
+            wait_bytes(ref.at[:, :, pl.ds(0, rows)], ring_s.at[n])
+
+    flush_sends()
     z_copy.wait_recv()
-    ow_out[...] = (rsum[:, own_lanes] + zin[...].astype(F32)) * NORM
-
-    run(1, NCTX, lambda d: o_copy(d, (c + d) % NCTX).wait_recv())
+    ow_buf[...] = (rsum[:, own_lanes] + zin[...].astype(F32)) * NORM
+    stores.append(pltpu.make_async_copy(ow_buf, ow_out, io.at[6]))
+    stores[3].start()
+
+    wait_bytes(yz_all.at[pl.ds(0, NCTX - 1)], o_r.at[0])
     scale = NORM * jnp.sqrt(2.0 * rate_rows)
     gain_sum = jnp.concatenate([yz_all[0:MODES, grp] for grp in range(GROUPS)], axis=1)
     rate_sum = jnp.concatenate([yz_all[MODES:2 * MODES, grp] for grp in range(GROUPS)], axis=1)
     gain_out[...] = scale * gain_sum
     rate_out[...] = scale * gain2[...] * (0.5 * gain_sum - rate_rows * rate_sum)
-    e_pair.wait_send()
-    q_pair.wait_send()
-    run(plane + 1, PLANE, lambda other: e_copy(other, plane).wait_send())
-    run(0, plane, lambda other: q_copy(other, plane).wait_send())
-    run(1, NCTX, lambda d: y_copy(d, c).wait_send())
-    run(1, NCTX, lambda d: o_copy(d, c).wait_send())
-    for copy in pending[OFF_O:]:
-        copy.wait_send()
+    wait_bytes(yz_all.at[pl.ds(0, NCTX - 1)], o_s.at[0])
+    for copy in stores:
+        copy.wait()
 
 
 def on_device(query_proj, key_proj, value_proj, filter_gains, log_rates, out_weight, grad_out):
     gain2 = filter_gains.T
     rate2 = log_rates.T
     vmem = pl.BlockSpec(memory_space=pltpu.VMEM)
+    hbm = pl.BlockSpec(memory_space=pl.ANY)
     shape = jax.ShapeDtypeStruct
     dma = pltpu.SemaphoreType.DMA
     wide = (MODES, SUB, CH)
@@ -742,9 +790,16 @@
             shape((MODES, CH), F32),
             shape((CH, 128), F32),
         ),
-        in_specs=[vmem] * 7,
-        out_specs=[vmem] * 6,
+        in_specs=[hbm, hbm, hbm, vmem, vmem, hbm, hbm],
+        out_specs=[hbm, hbm, hbm, vmem, vmem, hbm],
         scratch_shapes=[
+            pltpu.VMEM((ROWS, CH), BF16),
+            pltpu.VMEM((ROWS, CH), BF16),
+            pltpu.VMEM((ROWS, CH), BF16),
+            pltpu.VMEM((ROWS, CH), BF16),
+            pltpu.VMEM((ROWS, CH), BF16),
+            pltpu.VMEM((ROWS, CH), BF16),
+            pltpu.VMEM((CH, 128), F32),
             pltpu.VMEM((MODES, 1, CH), F32),
             pltpu.VMEM((4, 4, ROWS, 256), BF16),
             pltpu.VMEM((4, 4, CH, 256), BF16),
@@ -789,19 +844,20 @@
             pltpu.VMEM((CH, 256), F32),
             pltpu.VMEM((CH, 128), BF16),
             pltpu.VMEM((CH, 128), BF16),
-            dma((N_RING,)),
+            dma((3,)),
             dma((N_RING,)),
             dma((PLANE,)),
             dma((PLANE,)),
             dma((PLANE,)),
             dma((PLANE,)),
-            dma((NCTX,)),
-            dma((NCTX,)),
-            dma((NCTX,)),
-            dma((NCTX,)),
+            dma((1,)),
+            dma((1,)),
+            dma((1,)),
+            dma((1,)),
             dma((2,)),
             dma((2,)),
             dma((3,)),
+            dma((7,)),
         ],
         compiler_params=pltpu.CompilerParams(
             collective_id=0, has_side_effects=True, vmem_limit_bytes=56 * 1024 * 1024

time: 104 us -> 94.1 us (0.905)
  Pallas kernels: 95.7 us -> 86.3 us
    pallas_call x1, Pallas kernels: 95.7 us -> 86.3 us  [on_device(): pl.pallas_call(kernel, out_shape=(shape((ROWS, CH), BF16), shape((ROWS, C...]
where the time goes in v3:
time: 94.1 us; the launch traced here: 93 us
  Pallas kernels  86.3 us (92%)
  local copies, waits for them, and re-layouts  6.05 us (6%)
    pallas_call x1, Pallas kernels, on_device(): pl.pallas_call(kernel, out_shape=(shape((ROWS, CH), BF16), shape((ROWS, C...  86.3 us
    unnamed x16, local copies, waits for them, and re-layouts  6.05 us

profile of v3, /device:TPU:32, one launch (start us, length us, event | category | flops | bytes accessed | tf_op | source)
XLA Modules:
  0.0 93.0 jit_solution(6615335026023940979)
XLA Ops:
  0.6 86.3 %shard_map.118 = (bf16[512,512]{1,0:T(8,128)(2,1)}, bf16[512,512]{1,0:T(8,128)(2,1)}, bf16[512,512]{1,0:T(8,128)(2,1)}, f32[16,512]{1,0:T(8,128)}, f32[16,512]{1,0:T(8,128)}, /*index=5*/f32[512,128]{1,0:T(8,128)}) custom-call(bf16[512,512]{1,0:T(8,128)(2,1)} %q_in.1, bf16[512,512]{1,0:T(8,128)(2,1)} %k_in.1, bf16[512,512]{1,0:T(8,128)(2,1)} %v_in.1, ...), custom_call_target="tpu_custom_call" | custom-call | flops 5000000000 | bytes 5000000 | tf_op jit(solution)/shard_map/pallas_call | solution.py:783
  86.9 0.0 copy-start.1
  86.9 1.9 %copy.19 = bf16[512,512]{1,0:T(8,128)(2,1)} copy(bf16[512,512]{1,0:T(8,128)(2,1)} %get-tuple-element.24) | data formatting | bytes 1048576
  88.8 0.0 copy-done.1
  88.8 0.0 copy-start
  88.8 0.8 copy.20
  89.6 0.4 copy-done
  90.1 0.0 copy-start.4
  90.1 0.0 copy-start.2
  90.1 0.8 copy.21
  90.9 0.0 copy-done.4
  90.9 0.0 copy-start.3
  90.9 0.6 copy.22
  91.5 0.2 copy-done.3
  91.6 0.6 copy.23
  92.3 0.0 copy-done.2
  92.3 0.7 copy.24
Async XLA Ops:
  86.9 1.9 %copy-start.1 = (bf16[512,512]{1,0:T(8,128)(2,1)S(1)}, bf16[512,512]{1,0:T(8,128)(2,1)}, u32[]{:S(2)}) copy-start(bf16[512,512]{1,0:T(8,128)(2,1)} %get-tuple-element.25) | copy-start | bytes 1572868
  88.8 1.2 %copy-start = (bf16[512,512]{1,0:T(8,128)(2,1)S(1)}, bf16[512,512]{1,0:T(8,128)(2,1)}, u32[]{:S(2)}) copy-start(bf16[512,512]{1,0:T(8,128)(2,1)} %get-tuple-element.26) | copy-start | bytes 1572868
  90.1 0.8 copy-start.4
  90.1 2.2 %copy-start.2 = (f32[512,128]{1,0:T(8,128)S(1)}, f32[512,128]{1,0:T(8,128)}, u32[]{:S(2)}) copy-start(f32[512,128]{1,0:T(8,128)} %get-tuple-element.29) | copy-start | bytes 786436
  90.9 0.8 copy-start.3

commit v4 on v3

--- a/solution.py
+++ b/solution.py
@@ -24,12 +24,11 @@
 
 N_A = 36
 N_W = 45
-N_O = 6 * 4 + 6 + 6 + 6 + 1
+N_O = 6 * 4 + 6 + 6 + 6 + 2
 OFF_W = N_A
 OFF_O = OFF_W + N_W
 N_RING = OFF_O + N_O
 SENT_ROWS = (448, 496, 496)
-PLANE = 16
 W_SPLIT = 256
 
 
@@ -41,10 +40,10 @@
 
 
 def kernel(
-    q_in, k_in, v_in, gain2, rate2, w_ref, go_ref,
-    gq_out, gk_out, gv_out, gain_out, rate_out, ow_out,
-    q_ref, k_ref, v_ref, gq_buf, gk_buf, gv_buf, ow_buf, rate3, ag, wg, op, xs, gs, ys, perm, perm_t, a8, amp8,
-    ebuf, epeer, esend, eall, qbuf, qpeer, qsend, qall, hd3, st2,
+    q_in, k_in, v_in, gain_in, rate_in, w_ref, go_ref,
+    gq_out, ig_out, yz_out, ow_out,
+    q_ref, k_ref, v_ref, gain2, rate2, rate3, tkeep, ag, wg, op, xs, gs, ys, perm, perm_t, a8, amp8,
+    ebuf, epeer, esend, erow, eout, ecol, qbuf, qpeer, qsend, qrow, qout, qcol, hd3, st2,
     scr8, hfs, hft, hbwd, gate, cv, gt, yz, yz_in, yz_all,
     oppx, finx, vsum, oppy, finy, oppb, finb, vcol, oppv, finv, rsum, rsend, zin,
     ring_s, ring_r, e_s, e_r, q_s, q_r, y_s, y_r, o_s, o_r, pair_s, pair_r, loc, io,
@@ -56,7 +55,6 @@
     zl = c % 2
     zh = t // 2
     core = t % 2
-    plane = c // 2
 
     def ctx_of(xx, yy, zz):
         return xx * 8 + yy * 2 + zz
@@ -99,9 +97,11 @@
         pl.semaphore_signal(barrier, inc=1, device_id=(c, ten), device_id_type=MESH)
     loads = [
         pltpu.make_async_copy(src, dst, io.at[n])
-        for n, (src, dst) in enumerate([(k_in, k_ref), (v_in, v_ref), (q_in, q_ref)])
+        for n, (src, dst) in enumerate(
+            [(k_in, k_ref), (v_in, v_ref), (q_in, q_ref), (gain_in, gain2), (rate_in, rate2)]
+        )
     ]
-    for copy in loads:
+    for copy in reversed(loads):
         copy.start()
 
     pl.semaphore_wait(barrier, NCTX - 1 + 3)
@@ -179,6 +179,8 @@
         for copy in piece_par[k]:
             copy.wait_recv()
 
+    loads[3].wait()
+    loads[4].wait()
     rate_rows = jnp.exp(rate2[...])
     decay_rows = jnp.exp(-rate_rows)
     amp_rows = gain2[...] * jnp.sqrt(2.0 * rate_rows)
@@ -342,31 +344,59 @@
             for m in range(count):
                 st2[m:m + 1, grp * LANES:(grp + 1) * LANES] = scr8[grp, m, edge:edge + 1, :]
 
-    def scan_out(src, backward, start, group0, group1):
-        def group(grp):
-            decay = a8[:, :, lane_at(grp)]
-            amp = amp8[:, :, lane_at(grp)]
-
-            def step(i, state):
-                for u in range(UNROLL):
-                    j = i * UNROLL + u
-                    j = STEPS - 1 - j if backward else j
-                    state = decay * state + src[grp, step_rows(j)][None]
-                    ys[grp, step_rows(j)] = jnp.sum(amp * state, axis=0)
-                return state
-
-            lax.fori_loop(0, STEPS // UNROLL, step, start[:, :, lane_at(grp)])
-
-        run(group0, group1, group)
-
-    def exchange(src, dst, send, recv):
-        def make(other, index):
-            return pltpu.make_async_remote_copy(
-                src_ref=src, dst_ref=dst.at[index], send_sem=send.at[other],
-                recv_sem=recv.at[index], device_id=(other * 2 + zl, t), device_id_type=MESH,
-            )
-
-        return make
+    def scan_forward(grp):
+        decay = a8[:, :, lane_at(grp)]
+        amp = amp8[:, :, lane_at(grp)]
+
+        def step(i, carry):
+            state, timed = carry
+            for u in range(UNROLL):
+                j = i * UNROLL + u
+                decayed = decay * state
+                timed = decay * timed + decayed
+                state = decayed + xs[grp, step_rows(j)][None]
+                tkeep[grp, j] = timed
+                ys[grp, step_rows(j)] = jnp.sum(amp * state, axis=0)
+            return (state, timed)
+
+        lax.fori_loop(
+            0, STEPS // UNROLL, step, (hfs[:, :, lane_at(grp)], hft[:, :, lane_at(grp)])
+        )
+
+    def scan_backward(grp):
+        decay = a8[:, :, lane_at(grp)]
+        amp = amp8[:, :, lane_at(grp)]
+
+        def step(i, state):
+            for u in range(UNROLL):
+                j = STEPS - 1 - (i * UNROLL + u)
+                state = decay * state + gs[grp, step_rows(j)][None]
+                ys[grp, step_rows(j)] = jnp.sum(amp * state, axis=0)
+            return state
+
+        lax.fori_loop(0, STEPS // UNROLL, step, hbwd[:, :, lane_at(grp)])
+
+    def level_copy(src, dst, send, recv, ctx):
+        return pltpu.make_async_remote_copy(
+            src_ref=src, dst_ref=dst, send_sem=send, recv_sem=recv,
+            device_id=(ctx, t), device_id_type=MESH,
+        )
+
+    def row_copies(src, row, send, recv):
+        return [
+            level_copy(src, row.at[y], send.at[d], recv.at[y], ctx_of(x, (y + d) % 4, zl))
+            for d in range(1, 4)
+        ]
+
+    def row_wait(src, row, send, recv):
+        for d in range(1, 4):
+            other = (y + d) % 4
+            level_copy(src, row.at[other], send.at[d], recv.at[other], y_right).wait_recv()
+
+    def col_copy(src, col, send, recv, xx, index):
+        return level_copy(
+            src, col.at[index], send.at[4 + xx], recv.at[4 + index], ctx_of(xx, y, zl)
+        )
 
     def pair_copy(n, src, dst):
         return pltpu.make_async_remote_copy(
@@ -378,6 +408,8 @@
     one_decay = jnp.exp(-rate_rows * chunk)
     two_decay = jnp.exp(-rate_rows * (2.0 * chunk))
     odd = zl == 1
+    row_decay = jnp.exp(-rate_rows * (8.0 * chunk))
+    zero_rows = jnp.zeros((MODES, CH), F32)
 
     for copy in local:
         copy.wait()
@@ -393,15 +425,13 @@
     loads[1].wait()
     signal = (k_ref[...].astype(F32) * v_ref[...].astype(F32)).astype(BF16)
     spread(xs, signal)
-    run(0, 2, forward_group)
-    w_first()
-    run(2, GROUPS, forward_group)
+    run(0, GROUPS, forward_group)
     edge_rows(2 * MODES, SUB - 1)
     ebuf[...] = st2[...].astype(BF16)
     e_pair = pair_copy(0, ebuf, epeer)
     e_pair.start()
+    w_first()
     piece_start(1)
-    w_second()
     e_pair.wait_recv()
     peer = epeer[...].astype(F32)
     own = st2[...]
@@ -410,24 +440,45 @@
     first_s, first_t = first[:MODES], first[MODES:]
     esend[0:MODES] = (second[:MODES] + one_decay * first_s).astype(BF16)
     esend[MODES:] = (second[MODES:] + one_decay * (first_t + chunk * first_s)).astype(BF16)
-    e_copy = exchange(esend, eall, e_s, e_r)
-    run(plane + 1, PLANE, lambda other: e_copy(other, plane).start())
+    e_row = row_copies(esend, erow, e_s, e_r)
+    for copy in e_row:
+        copy.start()
+    erow[y] = esend[...]
+    w_second()
     piece_forward(0)
+
+    row_wait(esend, erow, e_s, e_r)
+    head_s, head_t, row_s, row_t = (zero_rows,) * 4
+    for yy in range(4):
+        rows = erow[yy].astype(F32)
+        ahead = yy < y
+        head_t = jnp.where(
+            ahead, two_decay * (head_t + 2.0 * chunk * head_s) + rows[MODES:], head_t
+        )
+        head_s = jnp.where(ahead, two_decay * head_s + rows[:MODES], head_s)
+        row_t = two_decay * (row_t + 2.0 * chunk * row_s) + rows[MODES:]
+        row_s = two_decay * row_s + rows[:MODES]
+    eout[0:MODES] = row_s.astype(BF16)
+    eout[MODES:] = row_t.astype(BF16)
+    run(x + 1, 4, lambda xx: col_copy(eout, ecol, e_s, e_r, xx, x).start())
+    piece_forward(1)
     w_third()
-    piece_forward(1)
-
-    run(0, plane, lambda other: e_copy(other, other).wait_recv())
+
+    run(0, x, lambda xx: col_copy(eout, ecol, e_s, e_r, xx, xx).wait_recv())
 
     def join_forward(j, carry):
-        head_s, head_t = carry
-        rows = eall[j].astype(F32)
+        far_s, far_t = carry
+        rows = ecol[j].astype(F32)
         return (
-            two_decay * head_s + rows[:MODES],
-            two_decay * (head_t + 2.0 * chunk * head_s) + rows[MODES:],
-        )
-
-    zero_rows = jnp.zeros((MODES, CH), F32)
-    head_s, head_t = lax.fori_loop(0, plane, join_forward, (zero_rows, zero_rows))
+            row_decay * far_s + rows[:MODES],
+            row_decay * (far_t + 8.0 * chunk * far_s) + rows[MODES:],
+        )
+
+    far_s, far_t = lax.fori_loop(0, x, join_forward, (zero_rows, zero_rows))
+    gap = y.astype(F32) * (2.0 * chunk)
+    gap_decay = jnp.exp(-rate_rows * gap)
+    head_s = head_s + gap_decay * far_s
+    head_t = head_t + gap_decay * (far_t + gap * far_s)
     head_t = jnp.where(odd, peer[MODES:] + one_decay * (head_t + chunk * head_s), head_t)
     head_s = jnp.where(odd, peer[:MODES] + one_decay * head_s, head_s)
     for m in range(MODES):
@@ -443,12 +494,7 @@
         hft[:, :, lane_at(grp)] += weight * (in_t + ids * in_s)
 
     run(0, GROUPS, incoming_forward)
-    w_fourth()
-    scan_out(xs, False, hfs, 0, 2)
-    piece_pass(0)
-    scan_out(xs, False, hfs, 2, GROUPS)
-    w_fifth()
-    piece_forward(2)
+    run(0, GROUPS, scan_forward)
     loads[2].wait()
     cv[...] = gather_back().astype(BF16)
     gated = (q_ref[...].astype(F32) * cv[...].astype(F32)).astype(BF16).astype(F32)
@@ -617,28 +663,33 @@
 
         run(0, 4, block)
 
-    piece_pass(1)
+    w_fourth()
+    piece_pass(0)
+    w_fifth()
+    piece_forward(2)
     piece_wait(0)
     out_piece(0)
+    piece_pass(1)
+    piece_wait(1)
+    out_piece(1)
     w_end()
     gate[...] = jnp.zeros_like(gate)
     gate_piece(0)
     piece_forward(3)
-    piece_wait(1)
-    out_piece(1)
+    piece_pass(2)
     gate_piece(1)
     out_add(0)
-    piece_pass(2)
-    along_right()
     piece_wait(2)
     out_piece(2)
-    out_add(1)
+    along_right()
+    along_left()
     gate_piece(2)
     piece_pass(3)
-    along_left()
+    out_add(1)
+    out_first()
     piece_wait(3)
     gate_piece(3)
-    out_first()
+    out_add(2)
 
     conv_grad = (gate[...] * q_ref[...].astype(F32)).astype(BF16)
     spread(gs, conv_grad)
@@ -654,21 +705,18 @@
             decay = a8[mode, :, lane_at(grp)]
 
             def step(i, carry):
-                state, timed, gain_sum, rate_sum = carry
+                state, gain_sum, rate_sum = carry
                 for u in range(UNROLL):
-                    rows = step_rows(i * UNROLL + u)
-                    grad = gs[grp, rows][None]
-                    decayed = decay * state
-                    timed = decay * timed + decayed
-                    state = decayed + xs[grp, rows][None]
+                    j = i * UNROLL + u
+                    grad = gs[grp, step_rows(j)][None]
+                    state = decay * state + xs[grp, step_rows(j)][None]
                     gain_sum = gain_sum + grad * state
-                    rate_sum = rate_sum + grad * timed
-                return (state, timed, gain_sum, rate_sum)
+                    rate_sum = rate_sum + grad * tkeep[grp, j, mode]
+                return (state, gain_sum, rate_sum)
 
             zero = jnp.zeros((8, SUB, LANES), F32)
-            _, _, gain_sum, rate_sum = lax.fori_loop(
-                0, STEPS // UNROLL, step,
-                (hfs[mode, :, lane_at(grp)], hft[mode, :, lane_at(grp)], zero, zero),
+            _, gain_sum, rate_sum = lax.fori_loop(
+                0, STEPS // UNROLL, step, (hfs[mode, :, lane_at(grp)], zero, zero)
             )
             scr8[grp, mode] = gain_sum
             scr8[grp, pl.ds(MODES + part * 8, 8)] = rate_sum
@@ -692,63 +740,76 @@
         weight = jnp.exp(-rates_at(grp) * (((SUB - 1.0) - ids) * float(STEPS)))
         hbwd[:, :, lane_at(grp)] += weight * hd3[0:MODES, :, lane_at(grp)]
 
-    out_piece(3)
-    out_add(2)
+    run(0, 1, gain_scan)
     q_pair.wait_recv()
     peer_q = qpeer[...].astype(F32)
     own_q = st2[0:MODES]
     first_q = jnp.where(odd, peer_q, own_q)
     second_q = jnp.where(odd, own_q, peer_q)
     qsend[...] = (first_q + one_decay * second_q).astype(BF16)
-    q_copy = exchange(qsend, qall, q_s, q_r)
-    run(0, plane, lambda other: q_copy(other, plane).start())
-
-    gq_buf[...] = (gate[...] * cv[...].astype(F32)).astype(BF16)
-    stores = [pltpu.make_async_copy(gq_buf, gq_out, io.at[3])]
-    stores[0].start()
-    out_second()
-    along_own()
-    run(0, 1, gain_scan)
-    out_add(3)
-    run(1, 3, gain_scan)
-    out_third()
-    run(3, GROUPS, gain_scan)
+    q_row = row_copies(qsend, qrow, q_s, q_r)
+    for copy in q_row:
+        copy.start()
+    qrow[y] = qsend[...]
+
+    gq_out[...] = (gate[...] * cv[...].astype(F32)).astype(BF16)
+    out_piece(3)
+    run(1, GROUPS, gain_scan)
+    row_wait(qsend, qrow, q_s, q_r)
+    tail, row_q = zero_rows, zero_rows
+    for yy in range(3, -1, -1):
+        rows = qrow[yy].astype(F32)
+        tail = jnp.where(yy > y, two_decay * tail + rows, tail)
+        row_q = two_decay * row_q + rows
+    qout[...] = row_q.astype(BF16)
+    run(0, x, lambda xx: col_copy(qout, qcol, q_s, q_r, xx, x).start())
     for grp in range(GROUPS):
         yz[:, grp] = jnp.sum(scr8[grp], axis=1)
     run(1, NCTX, lambda d: y_copy(d, c).start())
-    along_add()
-
-    run(plane + 1, PLANE, lambda other: q_copy(other, other).wait_recv())
-    tail = lax.fori_loop(
-        0, PLANE - 1 - plane,
-        lambda j, h: two_decay * h + qall[PLANE - 1 - j].astype(F32),
-        zero_rows,
+    out_second()
+    along_own()
+    out_add(3)
+    out_third()
+
+    run(x + 1, 4, lambda xx: col_copy(qout, qcol, q_s, q_r, xx, xx).wait_recv())
+    far_q = lax.fori_loop(
+        0, 3 - x, lambda j, h: row_decay * h + qcol[3 - j].astype(F32), zero_rows
     )
+    tail = tail + jnp.exp(-rate_rows * ((3 - y).astype(F32) * (2.0 * chunk))) * far_q
     tail = jnp.where(odd, tail, peer_q + one_decay * tail)
     for m in range(MODES):
         hd3[m] = tail[m:m + 1, :]
     run(0, GROUPS, incoming_backward)
-    scan_out(gs, True, hbwd, 0, 2)
-    out_last()
-    along_last()
-    rsend[...] = rsum[:, pl.ds(pl.multiple_of((1 - zl) * 128, 128), 128)].astype(BF16)
-    z_copy = remote(OFF_O + 42, rsend, zin, z_peer, t)
-    scan_out(gs, True, hbwd, 2, GROUPS)
+    run(0, 2, scan_backward)
+    along_add()
+    run(2, GROUPS, scan_backward)
+    ig_out[...] = gather_back().astype(BF16)
+    z_copies = []
+
+    def z_start(half):
+        rows = slice(half * 256, (half + 1) * 256)
+        rsend[rows] = rsum[
+            rows, pl.ds(pl.multiple_of((1 - zl) * 128, 128), 128)
+        ].astype(BF16)
+        z_copies.append(remote(
+            OFF_O + 42 + half, rsend.at[pl.ds(half * 256, 256)],
+            zin.at[pl.ds(half * 256, 256)], z_peer, t,
+        ))
+
     wait_bytes(yz_in.at[pl.ds(0, NCTX - 1)], y_r.at[0])
     yz_in[c] = yz[c]
     yz_all[c] = jnp.sum(yz_in[...], axis=0)
     run(1, NCTX, lambda d: o_copy(d, c).start())
-    input_grad = gather_back().astype(BF16).astype(F32)
-    gk_buf[...] = (input_grad * v_ref[...].astype(F32)).astype(BF16)
-    stores.append(pltpu.make_async_copy(gk_buf, gk_out, io.at[4]))
-    stores[1].start()
-    gv_buf[...] = (input_grad * k_ref[...].astype(F32)).astype(BF16)
-    stores.append(pltpu.make_async_copy(gv_buf, gv_out, io.at[5]))
-    stores[2].start()
+    out_last()
+    z_start(0)
+    along_last()
+    z_start(1)
 
     def flush_sends():
-        run(plane + 1, PLANE, lambda other: e_copy(other, plane).wait_send())
-        run(0, plane, lambda other: q_copy(other, plane).wait_send())
+        for copy in e_row + q_row:
+            copy.wait_send()
+        run(x + 1, 4, lambda xx: col_copy(eout, ecol, e_s, e_r, xx, x).wait_send())
+        run(0, x, lambda xx: col_copy(qout, qcol, q_s, q_r, xx, x).wait_send())
         wait_bytes(yz.at[pl.ds(0, NCTX - 1)], y_s.at[0])
         e_pair.wait_send()
         q_pair.wait_send()
@@ -756,20 +817,30 @@
             wait_bytes(ref.at[:, :, pl.ds(0, rows)], ring_s.at[n])
 
     flush_sends()
-    z_copy.wait_recv()
-    ow_buf[...] = (rsum[:, own_lanes] + zin[...].astype(F32)) * NORM
-    stores.append(pltpu.make_async_copy(ow_buf, ow_out, io.at[6]))
-    stores[3].start()
+    for copy in z_copies:
+        copy.wait_recv()
+    ow_out[...] = (rsum[:, own_lanes] + zin[...].astype(F32)) * NORM
 
     wait_bytes(yz_all.at[pl.ds(0, NCTX - 1)], o_r.at[0])
+    yz_out[...] = yz_all[...]
+    wait_bytes(yz_all.at[pl.ds(0, NCTX - 1)], o_s.at[0])
+
+
+def finish(
+    gq_in, ow_in, ig_ref, k_ref, v_ref, sums, gain2, rate2,
+    gq_out, gk_out, gv_out, gain_out, rate_out, ow_out,
+):
+    gq_out[...] = gq_in[...]
+    ow_out[...] = ow_in[...]
+    input_grad = ig_ref[...].astype(F32)
+    gk_out[...] = (input_grad * v_ref[...].astype(F32)).astype(BF16)
+    gv_out[...] = (input_grad * k_ref[...].astype(F32)).astype(BF16)
+    rate_rows = jnp.exp(rate2[...])
     scale = NORM * jnp.sqrt(2.0 * rate_rows)
-    gain_sum = jnp.concatenate([yz_all[0:MODES, grp] for grp in range(GROUPS)], axis=1)
-    rate_sum = jnp.concatenate([yz_all[MODES:2 * MODES, grp] for grp in range(GROUPS)], axis=1)
+    gain_sum = jnp.concatenate([sums[0:MODES, grp] for grp in range(GROUPS)], axis=1)
+    rate_sum = jnp.concatenate([sums[MODES:2 * MODES, grp] for grp in range(GROUPS)], axis=1)
     gain_out[...] = scale * gain_sum
     rate_out[...] = scale * gain2[...] * (0.5 * gain_sum - rate_rows * rate_sum)
-    wait_bytes(yz_all.at[pl.ds(0, NCTX - 1)], o_s.at[0])
-    for copy in stores:
-        copy.wait()
 
 
 def on_device(query_proj, key_proj, value_proj, filter_gains, log_rates, out_weight, grad_out):
@@ -780,27 +851,24 @@
     shape = jax.ShapeDtypeStruct
     dma = pltpu.SemaphoreType.DMA
     wide = (MODES, SUB, CH)
-    grad_query, grad_key, grad_value, grad_gains, grad_rates, grad_weight = pl.pallas_call(
+    gq_raw, input_grad, sums, ow_raw = pl.pallas_call(
         kernel,
         out_shape=(
             shape((ROWS, CH), BF16),
             shape((ROWS, CH), BF16),
-            shape((ROWS, CH), BF16),
-            shape((MODES, CH), F32),
-            shape((MODES, CH), F32),
+            shape((2 * MODES, GROUPS, LANES), F32),
             shape((CH, 128), F32),
         ),
-        in_specs=[hbm, hbm, hbm, vmem, vmem, hbm, hbm],
-        out_specs=[hbm, hbm, hbm, vmem, vmem, hbm],
+        in_specs=[hbm] * 7,
+        out_specs=[vmem] * 4,
         scratch_shapes=[
             pltpu.VMEM((ROWS, CH), BF16),
             pltpu.VMEM((ROWS, CH), BF16),
             pltpu.VMEM((ROWS, CH), BF16),
-            pltpu.VMEM((ROWS, CH), BF16),
-            pltpu.VMEM((ROWS, CH), BF16),
-            pltpu.VMEM((ROWS, CH), BF16),
-            pltpu.VMEM((CH, 128), F32),
+            pltpu.VMEM((MODES, CH), F32),
+            pltpu.VMEM((MODES, CH), F32),
             pltpu.VMEM((MODES, 1, CH), F32),
+            pltpu.VMEM((GROUPS, STEPS, MODES, SUB, LANES), F32),
             pltpu.VMEM((4, 4, ROWS, 256), BF16),
             pltpu.VMEM((4, 4, CH, 256), BF16),
             pltpu.VMEM((4, 4, CH, 256), BF16),
@@ -814,11 +882,15 @@
             pltpu.VMEM((2 * MODES, CH), BF16),
             pltpu.VMEM((2 * MODES, CH), BF16),
             pltpu.VMEM((2 * MODES, CH), BF16),
-            pltpu.VMEM((PLANE, 2 * MODES, CH), BF16),
+            pltpu.VMEM((4, 2 * MODES, CH), BF16),
+            pltpu.VMEM((2 * MODES, CH), BF16),
+            pltpu.VMEM((4, 2 * MODES, CH), BF16),
             pltpu.VMEM((MODES, CH), BF16),
             pltpu.VMEM((MODES, CH), BF16),
             pltpu.VMEM((MODES, CH), BF16),
-            pltpu.VMEM((PLANE, MODES, CH), BF16),
+            pltpu.VMEM((4, MODES, CH), BF16),
+            pltpu.VMEM((MODES, CH), BF16),
+            pltpu.VMEM((4, MODES, CH), BF16),
             pltpu.VMEM((2 * MODES, 1, CH), F32),
             pltpu.VMEM((2 * MODES, CH), F32),
             pltpu.VMEM((GROUPS, 2 * MODES, SUB, LANES), F32),
@@ -846,10 +918,10 @@
             pltpu.VMEM((CH, 128), BF16),
             dma((3,)),
             dma((N_RING,)),
-            dma((PLANE,)),
-            dma((PLANE,)),
-            dma((PLANE,)),
-            dma((PLANE,)),
+            dma((8,)),
+            dma((8,)),
+            dma((8,)),
+            dma((8,)),
             dma((1,)),
             dma((1,)),
             dma((1,)),
@@ -857,7 +929,7 @@
             dma((2,)),
             dma((2,)),
             dma((3,)),
-            dma((7,)),
+            dma((5,)),
         ],
         compiler_params=pltpu.CompilerParams(
             collective_id=0, has_side_effects=True, vmem_limit_bytes=56 * 1024 * 1024
@@ -868,6 +940,20 @@
     )(
         query_proj, key_proj, value_proj, gain2, rate2, out_weight, grad_out,
     )
+    grad_query, grad_key, grad_value, grad_gains, grad_rates, grad_weight = pl.pallas_call(
+        finish,
+        out_shape=(
+            shape((ROWS, CH), BF16),
+            shape((ROWS, CH), BF16),
+            shape((ROWS, CH), BF16),
+            shape((MODES, CH), F32),
+            shape((MODES, CH), F32),
+            shape((CH, 128), F32),
+        ),
+        in_specs=[vmem] * 8,
+        out_specs=[vmem] * 6,
+        compiler_params=pltpu.CompilerParams(vmem_limit_bytes=60 * 1024 * 1024),
+    )(gq_raw, ow_raw, input_grad, key_proj, value_proj, sums, gain2, rate2)
     return (grad_query, grad_key, grad_value, grad_gains.T, grad_rates.T, grad_weight)
 
 

time: 94.1 us -> 85.4 us (0.908)
  local copies, waits for them, and re-layouts: 6.05 us -> 0 us
  Pallas kernels: 86.3 us -> 83.7 us
    unnamed x16 -> x0, local copies, waits for them, and re-layouts: 6.05 us -> none
    pallas_call x1, Pallas kernels: 86.3 us -> 80.7 us  [on_device(): pl.pallas_call(kernel, out_shape=(shape((ROWS, CH), BF16), shape((ROWS, C...]
    pallas_call x0 -> x1, Pallas kernels: none -> 3.03 us  [on_device(): pl.pallas_call(finish, out_shape=(shape((ROWS, CH), BF16), shape((ROWS, C...]
where the time goes in v4:
time: 85.4 us; the launch traced here: 84.4 us
  Pallas kernels  83.7 us (98%)
    pallas_call x1, Pallas kernels, on_device(): pl.pallas_call(kernel, out_shape=(shape((ROWS, CH), BF16), shape((ROWS, C...  80.7 us
    pallas_call x1, Pallas kernels, on_device(): pl.pallas_call(finish, out_shape=(shape((ROWS, CH), BF16), shape((ROWS, C...  3.03 us

profile of v4, /device:TPU:32, one launch (start us, length us, event | category | flops | bytes accessed | tf_op | source)
XLA Modules:
  0.0 84.4 jit_solution(1424556367331489911)
XLA Ops:
  0.6 80.7 %shard_map.118 = (bf16[512,512]{1,0:T(8,128)(2,1)}, bf16[512,512]{1,0:T(8,128)(2,1)}, f32[32,4,128]{2,1,0:T(4,128)}, f32[512,128]{1,0:T(8,128)}) custom-call(bf16[512,512]{1,0:T(8,128)(2,1)} %q_in.1, bf16[512,512]{1,0:T(8,128)(2,1)} %k_ref.1, bf16[512,512]{1,0:T(8,128)(2,1)} %v_ref.1, f32[16,512]{1,0:T(8,128)} %bitcast.4, f32[16,512]{1,0:T(8,128)} %bitcast.6, ...), custom_call_target="tpu_custom_call" | custom-call | flops 5000000000 | bytes 5000000 | tf_op jit(solution)/shard_map/pallas_call | solution.py:854
  81.3 3.0 %shard_map.119 = (bf16[512,512]{1,0:T(8,128)(2,1)}, bf16[512,512]{1,0:T(8,128)(2,1)}, bf16[512,512]{1,0:T(8,128)(2,1)}, f32[16,512]{1,0:T(8,128)}, f32[16,512]{1,0:T(8,128)}, /*index=5*/f32[512,128]{1,0:T(8,128)}) custom-call(bf16[512,512]{1,0:T(8,128)(2,1)} %get-tuple-element.16.gq_in, f32[512,128]{1,0:T(8,128)} %get-tuple-element.17.ow_in, ...), custom_call_target="tpu_custom_call" | custom-call | tf_op jit(solution)/shard_map/pallas_call | solution.py:943

commit v5 on v4

--- a/solution.py
+++ b/solution.py
@@ -754,7 +754,9 @@
 
     gq_out[...] = (gate[...] * cv[...].astype(F32)).astype(BF16)
     out_piece(3)
-    run(1, GROUPS, gain_scan)
+    run(1, 2, gain_scan)
+    along_own()
+    run(2, GROUPS, gain_scan)
     row_wait(qsend, qrow, q_s, q_r)
     tail, row_q = zero_rows, zero_rows
     for yy in range(3, -1, -1):
@@ -767,7 +769,6 @@
         yz[:, grp] = jnp.sum(scr8[grp], axis=1)
     run(1, NCTX, lambda d: y_copy(d, c).start())
     out_second()
-    along_own()
     out_add(3)
     out_third()
 
@@ -780,10 +781,14 @@
     for m in range(MODES):
         hd3[m] = tail[m:m + 1, :]
     run(0, GROUPS, incoming_backward)
-    run(0, 2, scan_backward)
+    run(0, 1, scan_backward)
     along_add()
-    run(2, GROUPS, scan_backward)
-    ig_out[...] = gather_back().astype(BF16)
+    run(1, 3, scan_backward)
+    wait_bytes(yz_in.at[pl.ds(0, NCTX - 1)], y_r.at[0])
+    yz_in[c] = yz[c]
+    yz_all[c] = jnp.sum(yz_in[...], axis=0)
+    run(1, NCTX, lambda d: o_copy(d, c).start())
+    run(3, GROUPS, scan_backward)
     z_copies = []
 
     def z_start(half):
@@ -796,14 +801,11 @@
             zin.at[pl.ds(half * 256, 256)], z_peer, t,
         ))
 
-    wait_bytes(yz_in.at[pl.ds(0, NCTX - 1)], y_r.at[0])
-    yz_in[c] = yz[c]
-    yz_all[c] = jnp.sum(yz_in[...], axis=0)
-    run(1, NCTX, lambda d: o_copy(d, c).start())
     out_last()
     z_start(0)
     along_last()
     z_start(1)
+    ig_out[...] = gather_back().astype(BF16)
 
     def flush_sends():
         for copy in e_row + q_row:

time: 85.4 us -> 85.5 us (level)
  Pallas kernels: 83.7 us -> 84.7 us
    pallas_call x1, Pallas kernels: 80.7 us -> 81.7 us  [on_device(): pl.pallas_call(kernel, out_shape=(shape((ROWS, CH), BF16), shape((ROWS, C...]
where the time goes in v5:
time: 85.5 us; the launch traced here: 85.3 us
  Pallas kernels  84.7 us (99%)
    pallas_call x1, Pallas kernels, on_device(): pl.pallas_call(kernel, out_shape=(shape((ROWS, CH), BF16), shape((ROWS, C...  81.7 us
    pallas_call x1, Pallas kernels, on_device(): pl.pallas_call(finish, out_shape=(shape((ROWS, CH), BF16), shape((ROWS, C...  3.03 us

profile of v5, /device:TPU:32, one launch (start us, length us, event | category | flops | bytes accessed | tf_op | source)
XLA Modules:
  0.0 85.3 jit_solution(4567451794257410040)
XLA Ops:
  0.6 81.7 %shard_map.118 = (bf16[512,512]{1,0:T(8,128)(2,1)}, bf16[512,512]{1,0:T(8,128)(2,1)}, f32[32,4,128]{2,1,0:T(4,128)}, f32[512,128]{1,0:T(8,128)}) custom-call(bf16[512,512]{1,0:T(8,128)(2,1)} %q_in.1, bf16[512,512]{1,0:T(8,128)(2,1)} %k_ref.1, bf16[512,512]{1,0:T(8,128)(2,1)} %v_ref.1, f32[16,512]{1,0:T(8,128)} %bitcast.4, f32[16,512]{1,0:T(8,128)} %bitcast.6, ...), custom_call_target="tpu_custom_call" | custom-call | flops 5000000000 | bytes 5000000 | tf_op jit(solution)/shard_map/pallas_call | solution.py:856
  82.3 3.0 %shard_map.119 = (bf16[512,512]{1,0:T(8,128)(2,1)}, bf16[512,512]{1,0:T(8,128)(2,1)}, bf16[512,512]{1,0:T(8,128)(2,1)}, f32[16,512]{1,0:T(8,128)}, f32[16,512]{1,0:T(8,128)}, /*index=5*/f32[512,128]{1,0:T(8,128)}) custom-call(bf16[512,512]{1,0:T(8,128)(2,1)} %get-tuple-element.16.gq_in, f32[512,128]{1,0:T(8,128)} %get-tuple-element.17.ow_in, ...), custom_call_target="tpu_custom_call" | custom-call | tf_op jit(solution)/shard_map/pallas_call | solution.py:945

commit v6 on v4

--- a/solution.py
+++ b/solution.py
@@ -28,6 +28,7 @@
 OFF_W = N_A
 OFF_O = OFF_W + N_W
 N_RING = OFF_O + N_O
+N_RECV = N_RING - 12 - 15 - 12 - 9
 SENT_ROWS = (448, 496, 496)
 W_SPLIT = 256
 
@@ -42,7 +43,7 @@
 def kernel(
     q_in, k_in, v_in, gain_in, rate_in, w_ref, go_ref,
     gq_out, ig_out, yz_out, ow_out,
-    q_ref, k_ref, v_ref, gain2, rate2, rate3, tkeep, ag, wg, op, xs, gs, ys, perm, perm_t, a8, amp8,
+    q_ref, k_ref, v_ref, gain2, rate2, gq_buf, ig_buf, ow_buf, rate3, tkeep, ag, wg, op, xs, gs, ys, perm, perm_t, a8, amp8,
     ebuf, epeer, esend, erow, eout, ecol, qbuf, qpeer, qsend, qrow, qout, qcol, hd3, st2,
     scr8, hfs, hft, hbwd, gate, cv, gt, yz, yz_in, yz_all,
     oppx, finx, vsum, oppy, finy, oppb, finb, vcol, oppv, finv, rsum, rsend, zin,
@@ -68,10 +69,15 @@
     partner = zh * 2 + (1 - core)
     t_right, t_left = zp * 2 + core, zm * 2 + core
 
-    def remote(index, src, dst, ctx, ten):
+    ids = {}
+
+    def recv_sem(key):
+        return ring_r.at[ids.setdefault(key, len(ids))]
+
+    def remote(index, src, dst, ctx, ten, share=None):
         copy = pltpu.make_async_remote_copy(
             src_ref=src, dst_ref=dst, send_sem=ring_s.at[(index >= OFF_W) + (index >= OFF_O)],
-            recv_sem=ring_r.at[index],
+            recv_sem=recv_sem(index if share is None else share),
             device_id=(ctx, ten), device_id_type=MESH,
         )
         copy.start()
@@ -152,12 +158,12 @@
         lo = ag.at[zm, yk, duty_lo]
         f_r = remote(base + 2, lo, lo, c, t_right)
         full = ag.at[zm, yk, duty]
-        p_l = remote(base + 4, full, full, c, partner)
+        p_l = remote(base + 4, full, full, c, partner, ('p', k))
         from_right.wait_recv()
         hi = ag.at[zp, yk, duty_hi]
         f_l = remote(base + 3, hi, hi, c, t_left)
         full = ag.at[zp, yk, duty]
-        p_r = remote(base + 5, full, full, c, partner)
+        p_r = remote(base + 5, full, full, c, partner, ('p', k))
         piece_fwd[k] = (f_r, f_l)
         piece_par[k] = [p_l, p_r]
         if k + 2 < 4:
@@ -169,15 +175,14 @@
         f_r, f_l = piece_fwd[k]
         f_r.wait_recv()
         lo = ag.at[zo, yk, duty_lo]
-        p_a = remote(base + 6, lo, lo, c, partner)
+        p_a = remote(base + 6, lo, lo, c, partner, ('p', k))
         f_l.wait_recv()
         hi = ag.at[zo, yk, duty_hi]
-        p_b = remote(base + 7, hi, hi, c, partner)
+        p_b = remote(base + 7, hi, hi, c, partner, ('p', k))
         piece_par[k] += [p_a, p_b]
 
     def piece_wait(k):
-        for copy in piece_par[k]:
-            copy.wait_recv()
+        wait_bytes(ag.at[0, pl.ds(0, 2), pl.ds(0, 384)], recv_sem(('p', k)))
 
     loads[3].wait()
     loads[4].wait()
@@ -205,8 +210,8 @@
     wb = OFF_W + 1
     wc = {}
 
-    def w_send(index, ref, ctx):
-        return remote(wb + index, ref, ref, ctx, t)
+    def w_send(index, ref, ctx, share=None):
+        return remote(wb + index, ref, ref, ctx, t, share)
 
     def w_row(b, xb):
         wc["yr", b] = w_send(4 + 4 * b, wg.at[xb, y, w0], y_right)
@@ -214,9 +219,9 @@
 
     def w_row_forward(b, xb):
         wc["yr", b].wait_recv()
-        wc["yfr", b] = w_send(6 + 4 * b, wg.at[xb, ym, w0a], y_right)
+        wc["yfr", b] = w_send(6 + 4 * b, wg.at[xb, ym, w0a], y_right, 'w')
         wc["yl", b].wait_recv()
-        wc["yfl", b] = w_send(7 + 4 * b, wg.at[xb, yp, w0b], y_left)
+        wc["yfl", b] = w_send(7 + 4 * b, wg.at[xb, yp, w0b], y_left, 'w')
 
     def w_col(b, yb):
         wc["xr", b] = w_send(24 + 4 * b, wg.at[x, yb, w1], x_right)
@@ -224,9 +229,9 @@
 
     def w_col_forward(b, yb):
         wc["xr", b].wait_recv()
-        wc["xfr", b] = w_send(26 + 4 * b, wg.at[xm, yb, w1a], x_right)
+        wc["xfr", b] = w_send(26 + 4 * b, wg.at[xm, yb, w1a], x_right, 'w')
         wc["xl", b].wait_recv()
-        wc["xfl", b] = w_send(27 + 4 * b, wg.at[xp, yb, w1b], x_left)
+        wc["xfl", b] = w_send(27 + 4 * b, wg.at[xp, yb, w1b], x_left, 'w')
 
     def w_early():
         for n, (rows, ctx) in enumerate(((w0, x_right), (w0, x_left), (w1, y_right), (w1, y_left))):
@@ -281,9 +286,7 @@
         w_col_forward(3, yo)
 
     def w_end():
-        for b in range(4):
-            for name in ("yfr", "yfl", "xfr", "xfl"):
-                wc[name, b].wait_recv()
+        wait_bytes(wg.at[0], recv_sem('w'))
 
     w_early()
 
@@ -533,8 +536,8 @@
         far_l = remote(base + 1, unit(xo, 1), oppx.at[k, 1], x_left, t)
         rings[k] = [
             unit, far_r, far_l,
-            remote(base + 2, unit(xp, 1), finx.at[k, 0, 1], x_right, t),
-            remote(base + 3, unit(xm, 0), finx.at[k, 1, 0], x_left, t),
+            remote(base + 2, unit(xp, 1), finx.at[k, 0, 1], x_right, t, ('x', k)),
+            remote(base + 3, unit(xm, 0), finx.at[k, 1, 0], x_left, t, ('x', k)),
         ]
 
         def whole(part):
@@ -544,23 +547,22 @@
             along["far_r"] = remote(bbase, whole(0), oppb.at[0], y_right, t)
             along["far_l"] = remote(bbase + 1, whole(1), oppb.at[1], y_left, t)
         elif k == 1:
-            along["r1"] = remote(bbase + 2, whole(1), finb.at[0, 1], y_right, t)
+            along["r1"] = remote(bbase + 2, whole(1), finb.at[0, 1], y_right, t, 'b')
         elif k == 2:
-            along["l0"] = remote(bbase + 4, whole(0), finb.at[1, 0], y_left, t)
+            along["l0"] = remote(bbase + 4, whole(0), finb.at[1, 0], y_left, t, 'b')
 
     def along_right():
         along["far_r"].wait_recv()
         ref = add_into(op.at[:, order[1], part_b(0)], oppb[0])
-        along["r0"] = remote(bbase + 3, ref, finb.at[0, 0], y_right, t)
+        along["r0"] = remote(bbase + 3, ref, finb.at[0, 0], y_right, t, 'b')
 
     def along_left():
         along["far_l"].wait_recv()
         ref = add_into(op.at[:, order[2], part_b(1)], oppb[1])
-        along["l1"] = remote(bbase + 5, ref, finb.at[1, 1], y_left, t)
+        along["l1"] = remote(bbase + 5, ref, finb.at[1, 1], y_left, t, 'b')
 
     def along_own():
-        for name in ("r0", "r1", "l0", "l1"):
-            along[name].wait_recv()
+        wait_bytes(finb, recv_sem('b'))
         for part in range(2):
             rows = slice(part * 128, (part + 1) * 128)
             vcol[:, rows] = (
@@ -575,22 +577,21 @@
             unit,
             remote(vbase, unit(xo, 0), oppv.at[0], x_right, t),
             remote(vbase + 1, unit(xo, 1), oppv.at[1], x_left, t),
-            remote(vbase + 2, unit(xp, 1), finv.at[0, 1], x_right, t),
-            remote(vbase + 3, unit(xm, 0), finv.at[1, 0], x_left, t),
+            remote(vbase + 2, unit(xp, 1), finv.at[0, 1], x_right, t, 'v'),
+            remote(vbase + 3, unit(xm, 0), finv.at[1, 0], x_left, t, 'v'),
         ]
 
     def along_add():
         unit, far_r, far_l = along["ring"][:3]
         far_r.wait_recv()
         ref = add_into(unit(xp, 0), oppv[0])
-        along["ring"].append(remote(vbase + 4, ref, finv.at[0, 0], x_right, t))
+        along["ring"].append(remote(vbase + 4, ref, finv.at[0, 0], x_right, t, 'v'))
         far_l.wait_recv()
         ref = add_into(unit(xm, 1), oppv[1])
-        along["ring"].append(remote(vbase + 5, ref, finv.at[1, 1], x_left, t))
+        along["ring"].append(remote(vbase + 5, ref, finv.at[1, 1], x_left, t, 'v'))
 
     def along_last():
-        for copy in along["ring"][3:]:
-            copy.wait_recv()
+        wait_bytes(finv, recv_sem('v'))
         for part in range(2):
             rsum[256 + part * 128:256 + (part + 1) * 128] = (
                 vcol[x, part * 128:(part + 1) * 128].astype(F32) + finv[0, part].astype(F32)
@@ -602,15 +603,14 @@
         base = OFF_O + 6 * k
         far_r.wait_recv()
         ref = add_into(unit(xp, 0), oppx[k, 0])
-        rings[k].append(remote(base + 4, ref, finx.at[k, 0, 0], x_right, t))
+        rings[k].append(remote(base + 4, ref, finx.at[k, 0, 0], x_right, t, ('x', k)))
         far_l.wait_recv()
         ref = add_into(unit(xm, 1), oppx[k, 1])
-        rings[k].append(remote(base + 5, ref, finx.at[k, 1, 1], x_left, t))
+        rings[k].append(remote(base + 5, ref, finx.at[k, 1, 1], x_left, t, ('x', k)))
 
     def out_sum(k):
         unit = rings[k][0]
-        for copy in rings[k][3:]:
-            copy.wait_recv()
+        wait_bytes(finx.at[k], recv_sem(('x', k)))
         return [
             unit(x, part)[...].astype(F32) + finx[k, 0, part].astype(F32)
             + finx[k, 1, part].astype(F32)
@@ -629,23 +629,22 @@
     def out_second():
         parts = out_sum(1)
         vsum[1, 1] = parts[1].astype(BF16)
-        second_ring["r1"] = remote(ybase + 2, vsum.at[1, 1], finy.at[0, 1], y_right, t)
+        second_ring["r1"] = remote(ybase + 2, vsum.at[1, 1], finy.at[0, 1], y_right, t, 'y')
         second_ring["far_r"].wait_recv()
         vsum[1, 0] = (parts[0] + oppy[0].astype(F32)).astype(BF16)
-        second_ring["r0"] = remote(ybase + 3, vsum.at[1, 0], finy.at[0, 0], y_right, t)
+        second_ring["r0"] = remote(ybase + 3, vsum.at[1, 0], finy.at[0, 0], y_right, t, 'y')
 
     def out_third():
         parts = out_sum(2)
         vsum[2, 0] = parts[0].astype(BF16)
-        second_ring["l0"] = remote(ybase + 4, vsum.at[2, 0], finy.at[1, 0], y_left, t)
+        second_ring["l0"] = remote(ybase + 4, vsum.at[2, 0], finy.at[1, 0], y_left, t, 'y')
         second_ring["far_l"].wait_recv()
         vsum[2, 1] = (parts[1] + oppy[1].astype(F32)).astype(BF16)
-        second_ring["l1"] = remote(ybase + 5, vsum.at[2, 1], finy.at[1, 1], y_left, t)
+        second_ring["l1"] = remote(ybase + 5, vsum.at[2, 1], finy.at[1, 1], y_left, t, 'y')
 
     def out_last():
         parts = out_sum(3)
-        for name in ("r0", "r1", "l0", "l1"):
-            second_ring[name].wait_recv()
+        wait_bytes(finy, recv_sem('y'))
         for part in range(2):
             rsum[part * 128:(part + 1) * 128] = (
                 parts[part] + finy[0, part].astype(F32) + finy[1, part].astype(F32)
@@ -752,7 +751,9 @@
         copy.start()
     qrow[y] = qsend[...]
 
-    gq_out[...] = (gate[...] * cv[...].astype(F32)).astype(BF16)
+    gq_buf[...] = (gate[...] * cv[...].astype(F32)).astype(BF16)
+    stores = [pltpu.make_async_copy(gq_buf, gq_out, io.at[5])]
+    stores[0].start()
     out_piece(3)
     run(1, GROUPS, gain_scan)
     row_wait(qsend, qrow, q_s, q_r)
@@ -783,7 +784,9 @@
     run(0, 2, scan_backward)
     along_add()
     run(2, GROUPS, scan_backward)
-    ig_out[...] = gather_back().astype(BF16)
+    ig_buf[...] = gather_back().astype(BF16)
+    stores.append(pltpu.make_async_copy(ig_buf, ig_out, io.at[6]))
+    stores[1].start()
     z_copies = []
 
     def z_start(half):
@@ -817,13 +820,18 @@
             wait_bytes(ref.at[:, :, pl.ds(0, rows)], ring_s.at[n])
 
     flush_sends()
+    assert len(ids) == N_RECV
     for copy in z_copies:
         copy.wait_recv()
-    ow_out[...] = (rsum[:, own_lanes] + zin[...].astype(F32)) * NORM
+    ow_buf[...] = (rsum[:, own_lanes] + zin[...].astype(F32)) * NORM
+    stores.append(pltpu.make_async_copy(ow_buf, ow_out, io.at[7]))
+    stores[2].start()
 
     wait_bytes(yz_all.at[pl.ds(0, NCTX - 1)], o_r.at[0])
     yz_out[...] = yz_all[...]
     wait_bytes(yz_all.at[pl.ds(0, NCTX - 1)], o_s.at[0])
+    for copy in stores:
+        copy.wait()
 
 
 def finish(
@@ -860,13 +868,16 @@
             shape((CH, 128), F32),
         ),
         in_specs=[hbm] * 7,
-        out_specs=[vmem] * 4,
+        out_specs=[hbm, hbm, vmem, hbm],
         scratch_shapes=[
             pltpu.VMEM((ROWS, CH), BF16),
             pltpu.VMEM((ROWS, CH), BF16),
             pltpu.VMEM((ROWS, CH), BF16),
             pltpu.VMEM((MODES, CH), F32),
             pltpu.VMEM((MODES, CH), F32),
+            pltpu.VMEM((ROWS, CH), BF16),
+            pltpu.VMEM((ROWS, CH), BF16),
+            pltpu.VMEM((CH, 128), F32),
             pltpu.VMEM((MODES, 1, CH), F32),
             pltpu.VMEM((GROUPS, STEPS, MODES, SUB, LANES), F32),
             pltpu.VMEM((4, 4, ROWS, 256), BF16),
@@ -917,7 +928,7 @@
             pltpu.VMEM((CH, 128), BF16),
             pltpu.VMEM((CH, 128), BF16),
             dma((3,)),
-            dma((N_RING,)),
+            dma((N_RECV,)),
             dma((8,)),
             dma((8,)),
             dma((8,)),
@@ -929,7 +940,7 @@
             dma((2,)),
             dma((2,)),
             dma((3,)),
-            dma((5,)),
+            dma((8,)),
         ],
         compiler_params=pltpu.CompilerParams(
             collective_id=0, has_side_effects=True, vmem_limit_bytes=56 * 1024 * 1024

time: 85.4 us -> 84.8 us (level)
  no operation moved by 1% of the time
where the time goes in v6:
time: 84.8 us; the launch traced here: 83.7 us
  Pallas kernels  83.1 us (98%)
    pallas_call x1, Pallas kernels, on_device(): pl.pallas_call(kernel, out_shape=(shape((ROWS, CH), BF16), shape((ROWS, C...  80.1 us
    pallas_call x1, Pallas kernels, on_device(): pl.pallas_call(finish, out_shape=(shape((ROWS, CH), BF16), shape((ROWS, C...  3.03 us

profile of v6, /device:TPU:32, one launch (start us, length us, event | category | flops | bytes accessed | tf_op | source)
XLA Modules:
  0.0 83.7 jit_solution(3168253347929079193)
XLA Ops:
  0.6 80.1 %shard_map.118 = (bf16[512,512]{1,0:T(8,128)(2,1)}, bf16[512,512]{1,0:T(8,128)(2,1)}, f32[32,4,128]{2,1,0:T(4,128)}, f32[512,128]{1,0:T(8,128)}) custom-call(bf16[512,512]{1,0:T(8,128)(2,1)} %q_in.1, bf16[512,512]{1,0:T(8,128)(2,1)} %k_ref.1, bf16[512,512]{1,0:T(8,128)(2,1)} %v_ref.1, f32[16,512]{1,0:T(8,128)} %bitcast.4, f32[16,512]{1,0:T(8,128)} %bitcast.6, ...), custom_call_target="tpu_custom_call" | custom-call | flops 5000000000 | bytes 5000000 | tf_op jit(solution)/shard_map/pallas_call | solution.py:862
  80.7 3.0 %shard_map.119 = (bf16[512,512]{1,0:T(8,128)(2,1)}, bf16[512,512]{1,0:T(8,128)(2,1)}, bf16[512,512]{1,0:T(8,128)(2,1)}, f32[16,512]{1,0:T(8,128)}, f32[16,512]{1,0:T(8,128)}, /*index=5*/f32[512,128]{1,0:T(8,128)}) custom-call(bf16[512,512]{1,0:T(8,128)(2,1)} %get-tuple-element.16.gq_in, f32[512,128]{1,0:T(8,128)} %get-tuple-element.17.ow_in, ...), custom_call_target="tpu_custom_call" | custom-call | tf_op jit(solution)/shard_map/pallas_call | solution.py:954
